TPU v7x, 32 devices: a whole 2x2x4 slice. The times are simulated.
32 devices in a mesh: row: 4 (over y, x), col: 8 (over z, core).
Axes of the slice: x: 2, y: 2, z: 4, core: 2. Of those that a mesh axis runs over, the one named last changes fastest.
Arguments:
- grad: float32 [7168, 8192], P(('row', 'col')), may hold values from -60 to 60
- momentum: float32 [7168, 8192], P(('row', 'col')), may hold values from -6 to 6
Outputs:
- update: bfloat16 [7168, 8192], P(('row', 'col'))
- new_momentum: float32 [7168, 8192], P(('row', 'col'))
All inputs are finite; a program needn't handle non-finite values.
Results may differ from a plain program's by a relative error of at most 0.02.
Values may be sent and summed in bfloat16 or wider, within the bound.
No kernel may reach another device: no remote copies, remote signals or barrier semaphores. Data moves between devices by JAX's collectives and lax.ppermute only.
A program may use at most 128 MiB of HBM per device.

v0:
```python
import math

import jax
import jax.numpy as jnp
from jax import lax
from jax.sharding import PartitionSpec as P

M = 7168
N = 8192


momentum_coef = 0.95
rms_target = 0.4
coef_a = 3.4445
coef_b = -4.775
coef_c = 2.0315
inner_dims = (((1,), (1,)), ((), ()))
outer_dims = (((0,), (0,)), ((), ()))


def shards(grad, momentum):
    new_momentum = momentum_coef * momentum + grad
    direction = grad + momentum_coef * new_momentum
    sumsq = lax.psum(jnp.sum(direction * direction), ("row", "col"))
    factor = rms_target * math.sqrt(M) / (jnp.sqrt(sumsq) + 1e-07)
    start_rows = (direction * factor).astype(jnp.bfloat16)
    grid_block = lax.all_to_all(start_rows, "col", split_axis=1, concat_axis=0, tiled=True)
    full_panel = lax.all_gather(grid_block, "row", axis=0, tiled=True)
    block_rows = grid_block.shape[0]
    half_rows = block_rows // 2
    pieces = []
    for part_index in range(2):
        own_rows = grid_block[part_index * half_rows : (part_index + 1) * half_rows]

        def gram_term_rows(row_start, row_count, own_rows=own_rows):
            return lax.dot_general(
                full_panel, own_rows, inner_dims, preferred_element_type=jnp.float32
            )

        share_rows = full_panel.shape[0] // lax.axis_size("col")
        summed = lax.psum_scatter(
            gram_term_rows(jnp.int32(0), share_rows * lax.axis_size("col")).astype(jnp.bfloat16),
            "col",
            scatter_dimension=0,
            tiled=True,
        )
        pieces.append(summed)
    joined = jnp.concatenate(pieces, axis=1)
    gram_panel = lax.all_gather(joined, "col", axis=0, tiled=True)
    first = lax.dot_general(gram_panel, full_panel, outer_dims, preferred_element_type=jnp.float32)
    first_round = first.astype(jnp.bfloat16)
    second = lax.dot_general(
        gram_panel,
        lax.all_gather(first_round, "row", axis=0, tiled=True),
        outer_dims,
        preferred_element_type=jnp.float32,
    )
    scale_out = 0.2 * math.sqrt(max(M, N))
    result = coef_a * grid_block.astype(jnp.float32) + coef_b * first + coef_c * second
    update_block = (result * scale_out).astype(jnp.bfloat16)
    update = lax.all_to_all(update_block, "col", split_axis=0, concat_axis=1, tiled=True)
    return (update, new_momentum)


def solution(mesh):
    return jax.shard_map(
        shards,
        mesh=mesh,
        in_specs=(P(("row", "col"), None), P(("row", "col"), None)),
        out_specs=(P(("row", "col"), None), P(("row", "col"), None)),
        check_vma=False,
    )
```

profile of v0, /device:TPU:9, one launch (start us, length us, event | category | flops | bytes accessed | tf_op | source)
XLA Modules:
  0.0 1104.4 jit_solution(8349453941293854285)
XLA Ops:
  7.2 0.0 all-gather.4.cloned.1.call-start
  7.2 8.8 multiply_reduce_fusion
  16.0 40.1 %psum.7 = f32[]{:T(128)} all-reduce(f32[]{:T(128)} %get-tuple-element.2), channel_id=1, replica_groups=mesh['row'=4,'col'=8] {'row','col'}, use_global_device_ids=true, to_apply=%region_1.0 | all-reduce | flops 1 | bytes 8 | tf_op jit(solution)/shard_map/psum | solution.py:24
  56.8 6.5 multiply_convert_fusion.1
  63.3 0.4 copy.9
  63.7 84.6 %all_to_all.38 = bf16[224,8,1024]{2,0,1:T(8,128)(2,1)} all-to-all(bf16[224,8,1024]{2,0,1:T(8,128)(2,1)S(1)} %bitcast.24), channel_id=1, replica_groups=mesh['row'=4,'col'=8] {'col'}, dimensions={1} | all-to-all | bytes 7340032 | tf_op jit(solution)/shard_map/all_to_all | solution.py:27
  148.4 0.0 all-gather.4.cloned.1.call-update
  148.4 0.0 reduce-scatter.5.cloned.1.call-start
  148.4 3.8 fusion
  152.3 137.4 %all-gather.4.cloned.1.call-done = bf16[7168,1024]{1,0:T(8,128)(2,1)} async-done(((bf16[1792,1024]{1,0:T(8,128)(2,1)}), bf16[7168,1024]{1,0:T(8,128)(2,1)}) %all-gather.4.cloned.1.call-update) | async-done | bytes 14680080 | tf_op jit(solution)/shard_map/all_gather | solution.py:28
  289.7 21.0 %convolution_convert_fusion = bf16[7168,896]{1,0:T(8,128)(2,1)} fusion(bf16[7168,1024]{1,0:T(8,128)(2,1)} %all-gather.4.cloned.1.call-done, bf16[896,1024]{1,0:T(8,128)(2,1)} %bitcast.30), kind=kOutput, calls=%fused_computation | convolution fusion | flops 13159759872 | bytes 29360128 | tf_op jit(solution)/shard_map/dot_general | solution.py:36
  310.7 0.2 reduce-scatter.3.cloned.1.call-start
  310.9 22.7 %convolution_convert_fusion.1 = bf16[7168,896]{1,0:T(8,128)(2,1)} fusion(bf16[7168,1024]{1,0:T(8,128)(2,1)} %all-gather.4.cloned.1.call-done, bf16[896,1024]{1,0:T(8,128)(2,1)S(1)} %bitcast.29), kind=kOutput, calls=%fused_computation.1 | convolution fusion | flops 13159759872 | bytes 29360128 | tf_op jit(solution)/shard_map/dot_general | solution.py:36
  333.7 0.0 all-gather.6.cloned.1.call-start
  333.7 107.3 %reduce-scatter.5.cloned.1.call-done = bf16[896,896]{1,0:T(8,128)(2,1)} async-done(((bf16[7168,896]{1,0:T(8,128)(2,1)}), bf16[896,896]{1,0:T(8,128)(2,1)}) %reduce-scatter.5.cloned.1.call-update) | async-done | bytes 1605648 | tf_op jit(solution)/shard_map/reduce_scatter | solution.py:41
  441.0 132.4 %reduce-scatter.3.cloned.1.call-done = bf16[896,896]{1,0:T(8,128)(2,1)} async-done(((bf16[7168,896]{1,0:T(8,128)(2,1)}), bf16[896,896]{1,0:T(8,128)(2,1)}) %reduce-scatter.3.cloned.1.call-update) | async-done | bytes 1605648 | tf_op jit(solution)/shard_map/reduce_scatter | solution.py:41
  573.4 3.8 pad_maximum_fusion
  577.3 0.0 all-gather.8.cloned.1.call-start
  577.3 221.6 %all-gather.6.cloned.1.call-done = bf16[7168,1792]{1,0:T(8,128)(2,1)} async-done(((bf16[896,1792]{1,0:T(8,128)(2,1)}), bf16[7168,1792]{1,0:T(8,128)(2,1)}) %all-gather.6.cloned.1.call-update) | async-done | bytes 25690128 | tf_op jit(solution)/shard_map/all_gather | solution.py:49
  798.9 35.4 %fusion.1 = (bf16[1792,1024]{1,0:T(8,128)(2,1)}, f32[1792,1024]{1,0:T(8,128)}) fusion(bf16[7168,1792]{1,0:T(8,128)(2,1)} %all-gather.6.cloned.1.call-done, bf16[7168,1024]{1,0:T(8,128)(2,1)} %all-gather.4.cloned.1.call-done), kind=kOutput, calls=%fused_computation.10 | convolution fusion | flops 26308509696 | bytes 51380224 | tf_op jit(solution)/shard_map/dot_general | solution.py:50
  834.3 140.9 %all-gather.8.cloned.1.call-done = bf16[7168,1024]{1,0:T(8,128)(2,1)} async-done(((bf16[1792,1024]{1,0:T(8,128)(2,1)}), bf16[7168,1024]{1,0:T(8,128)(2,1)}) %all-gather.8.cloned.1.call-update) | async-done | bytes 14680080 | tf_op jit(solution)/shard_map/all_gather | solution.py:54
  975.2 35.5 %multiply_convert_fusion = bf16[1792,1024]{1,0:T(8,128)(2,1)S(1)} fusion(f32[1792,1024]{1,0:T(8,128)} %get-tuple-element.7, bf16[1792,1024]{1,0:T(8,128)(2,1)} %bitcast.23, bf16[7168,1792]{1,0:T(8,128)(2,1)} %all-gather.6.cloned.1.call-done, bf16[7168,1024]{1,0:T(8,128)(2,1)} %all-gather.8.cloned.1.call-done), kind=kOutput, calls=%fused_computation.2 | convolution fusion | flops 26321354752 | bytes 55050240 | tf_op jit(solution)/shard_map/dot_general | solution.py:52
  1010.7 84.9 %all_to_all.39 = bf16[8,224,1024]{2,1,0:T(8,128)(2,1)S(1)} all-to-all(bf16[8,224,1024]{2,1,0:T(8,128)(2,1)S(1)} %bitcast.27), channel_id=1, replica_groups=mesh['row'=4,'col'=8] {'col'}, dimensions={0} | all-to-all | bytes 7340032 | tf_op jit(solution)/shard_map/all_to_all | solution.py:61
  1095.6 2.3 copy.7
  (4 shorter events, 0.1 us)
Async XLA Ops:
  7.2 282.5 %all-gather.4.cloned.1.call-start = ((), (), s32[]{:S(2)}) async-start(), calls=%async_computation.4 | async-start | bytes 18350080 | tf_op jit(solution)/shard_map/all_gather | solution.py:28
  148.4 292.6 %reduce-scatter.5.cloned.1.call-start = ((), (), s32[]{:S(2)}) async-start(), calls=%async_computation.6 | async-start | bytes 14450688 | tf_op jit(solution)/shard_map/reduce_scatter | solution.py:41
  310.7 262.7 %reduce-scatter.3.cloned.1.call-start = ((), (), s32[]{:S(2)}) async-start(), calls=%async_computation.5 | async-start | bytes 14450688 | tf_op jit(solution)/shard_map/reduce_scatter | solution.py:41
  333.7 465.2 %all-gather.6.cloned.1.call-start = ((), (), s32[]{:S(2)}) async-start(), calls=%async_computation.7 | async-start | bytes 28901376 | tf_op jit(solution)/shard_map/all_gather | solution.py:49
  577.3 397.9 %all-gather.8.cloned.1.call-start = ((), (), s32[]{:S(2)}) async-start(), calls=%async_computation.8 | async-start | bytes 18350080 | tf_op jit(solution)/shard_map/all_gather | solution.py:54
Sparse Core Ops, SparseCore 0:
  148.5 141.1 all-gather.3
  310.8 130.1 reduce-scatter.4
  443.4 130.0 reduce-scatter.2
  577.4 221.4 all-gather.5
  834.4 140.7 all-gather.7
where the time goes:
time: 1110 us; the launch traced here: 1100 us
  waiting for transfers between devices  740 us (67%)
  blocking collectives  210 us (19%)
  matrix products  115 us (10%)
  other arithmetic  19.1 us (2%)
  between operations  14.5 us (1%)
    reduce_scatter x2, waiting for transfers between devices, shards(): lax.psum_scatter(gram_term_rows(jnp.int32(0), share_rows * lax.axis_size(...  240 us
    all_gather x1, waiting for transfers between devices, shards(): gram_panel = lax.all_gather(joined, 'col', axis=0, tiled=True)  222 us
    all_gather x1, waiting for transfers between devices, shards(): lax.all_gather(first_round, 'row', axis=0, tiled=True)  141 us
    all_gather x1, waiting for transfers between devices, shards(): full_panel = lax.all_gather(grid_block, 'row', axis=0, tiled=True)  137 us
    all_to_all x1, blocking collectives, shards(): lax.all_to_all(update_block, 'col', split_axis=0, concat_axis=1, tiled=True)  84.9 us
    all_to_all x1, blocking collectives, shards(): lax.all_to_all(start_rows, 'col', split_axis=1, concat_axis=0, tiled=True)  84.6 us
    dot_general x2, matrix products, gram_term_rows(): lax.dot_general(full_panel, own_rows, inner_dims, preferred_element_type=...  43.7 us
    psum x1, blocking collectives, shards(): sumsq = lax.psum(jnp.sum(direction * direction), ('row', 'col'))  40.1 us
  transfers between devices with their start and end apart: 5, of which 5 were waited for; matrix products, arithmetic and copies ran while one was open for 2% of the time, Pallas kernels for 0%

commit v1 on v0

v1 whole, which is shorter than its diff:
```python
import math

import jax
import jax.numpy as jnp
from jax import lax
from jax.sharding import PartitionSpec as P

momentum_coef = 0.95
rms_target = 0.4
coef_a = 3.4445
coef_b = -4.775
coef_c = 2.0315
CHUNKS = 2
F32 = jnp.float32
BF16 = jnp.bfloat16


def xor_pairs(size, distance):
    return [(i, i ^ distance) for i in range(size)]


def shift_pairs(size, distance):
    return [(i, (i + distance) % size) for i in range(size)]


def low_bit(distance):
    return (distance & -distance).bit_length() - 1


def shards(grad, momentum):
    n_row, n_col = lax.axis_size("row"), lax.axis_size("col")
    n_ring = n_col // 2
    row, col = lax.axis_index("row"), lax.axis_index("col")
    ring, core = col // 2, col % 2
    rows, n_in = grad.shape
    half = rows // 2
    width = n_in // n_col
    tall = half * n_col
    m_total = rows * n_row * n_col

    def across(value, distance):
        return lax.ppermute(value, "row", xor_pairs(n_row, distance))

    def other_core(value):
        return lax.ppermute(value, "col", xor_pairs(n_col, 1))

    def next_in_ring(value):
        return lax.ppermute(value, "col", shift_pairs(n_col, 2))

    new_momentum = momentum_coef * momentum + grad
    direction = grad + momentum_coef * new_momentum
    raw = direction.astype(BF16)

    sumsq = jnp.sum(direction * direction).reshape(1, 1)
    step = 1
    while step < n_col:
        sumsq = sumsq + lax.ppermute(sumsq, "col", xor_pairs(n_col, step))
        step *= 2
    step = 1
    while step < n_row:
        sumsq = sumsq + across(sumsq, step)
        step *= 2
    factor = rms_target * math.sqrt(m_total) / (jnp.sqrt(sumsq) + 1e-07)
    factor_sq = (factor * factor).reshape(1, 1, 1)

    own, others = [], [{}, {}]
    for h in range(2):
        block = lax.all_to_all(
            raw[h * half : (h + 1) * half], "col", split_axis=1, concat_axis=0, tiled=True
        )
        own.append(block)
        if n_row == 4:
            others[h][1] = across(block, 1)
            others[h][2] = across(block, 2)
            others[h][3] = across(others[h][1], 2) if h == 0 else across(others[h][2], 1)
        else:
            for d in range(1, n_row):
                others[h][d] = across(block, d)

    def swapped(first_half, second_half, d):
        upper = ((row >> low_bit(d)) & 1) == 1
        return jnp.stack(
            [
                jnp.where(upper, second_half, first_half),
                jnp.where(upper, first_half, second_half),
            ]
        )

    own2 = jnp.stack(own)
    mixed = {d: swapped(others[0][d], others[1][d], d) for d in range(1, n_row)}

    def gram_term(left, right):
        term = lax.dot_general(left, right, (((2,), (2,)), ((0,), (0,))), preferred_element_type=F32)
        return (term * factor_sq).astype(BF16)

    def reduce_ring(term):
        count = term.shape[0]
        pieces = term.reshape(count, n_ring, 2, half, tall)
        kept = lax.dynamic_index_in_dim(pieces, core, 2, keepdims=False)
        sent = lax.dynamic_index_in_dim(pieces, 1 - core, 2, keepdims=False)
        summed = (kept.astype(F32) + other_core(sent).astype(F32)).astype(BF16)

        def part(index):
            return lax.dynamic_index_in_dim(summed, index % n_ring, 1, keepdims=False)

        total = part(ring + n_ring - 1)
        for t in range(1, n_ring):
            total = next_in_ring(total).astype(F32) + part(ring + n_ring - 1 - t).astype(F32)
            total = total.astype(BF16)
        return total

    def gather_ring(piece):
        found = [piece]
        for _ in range(1, n_ring):
            found.append(next_in_ring(found[-1]))
        return found

    def assemble(found):
        count = found[0].shape[0]
        full = jnp.zeros((count, n_ring, 2, half, tall), BF16)
        partner = other_core(jnp.stack(found))
        for k, piece in enumerate(found):
            place = (ring - k + n_ring) % n_ring
            full = lax.dynamic_update_slice(full, piece[:, None, None], (0, place, core, 0, 0))
            full = lax.dynamic_update_slice(
                full, partner[k][:, None, None], (0, place, 1 - core, 0, 0)
            )
        return full.reshape(count, tall, tall)

    def exchange(found, d):
        upper = ((row >> low_bit(d)) & 1) == 1
        return [across(jnp.where(upper, piece[::-1], piece), d) for piece in found]

    corner = gather_ring(reduce_ring(gram_term(own2, own2)))
    side = gather_ring(reduce_ring(gram_term(own2[:1], own2[1:])))
    corner, side = assemble(corner), assemble(side)[0]
    near, far = {}, {}
    for d in range(1, n_row):
        found = gather_ring(reduce_ring(gram_term(own2, mixed[d])))
        near[d] = assemble(found)
        far[d] = assemble(exchange(found, d))

    def times_gram(mine, theirs):
        plain = (((2,), (1,)), ((0,), (0,)))
        turned = (((1,), (1,)), ((0,), (0,)))
        total = lax.dot_general(corner, mine, plain, preferred_element_type=F32)
        total = total + jnp.stack(
            [
                lax.dot_general(side, mine[1], (((1,), (0,)), ((), ())), preferred_element_type=F32),
                lax.dot_general(side, mine[0], (((0,), (0,)), ((), ())), preferred_element_type=F32),
            ]
        )
        for d in range(1, n_row):
            total = total + lax.dot_general(near[d], theirs[d], plain, preferred_element_type=F32)
            total = total + lax.dot_general(
                far[d], theirs[d][::-1], turned, preferred_element_type=F32
            )
        return total

    scale_out = 0.2 * math.sqrt(max(m_total, n_in))
    update = jnp.zeros((rows, n_in), BF16)
    part_width = width // CHUNKS
    for chunk in range(CHUNKS):
        cut = slice(chunk * part_width, (chunk + 1) * part_width)
        mine = own2[:, :, cut]
        first = times_gram(mine, {d: mixed[d][:, :, cut] for d in mixed})
        rounded = first.astype(BF16)
        if n_row == 4:
            got1, got2 = across(rounded, 1), across(rounded, 2)
            got = {1: got1, 2: got2, 3: (across(got1[0], 2), across(got2[1], 1))}
        else:
            got = {d: across(rounded, d) for d in range(1, n_row)}
        second = times_gram(rounded, {d: swapped(got[d][0], got[d][1], d) for d in got})
        result = coef_a * mine.astype(F32) + coef_b * first + coef_c * second
        block = (result * (factor * scale_out).reshape(1, 1, 1)).astype(BF16)
        block = block.reshape(2, n_col, half, part_width)
        for k in range(n_col):
            piece = lax.dynamic_index_in_dim(block, (col + k) % n_col, 1, keepdims=False)
            if k:
                piece = lax.ppermute(piece, "col", shift_pairs(n_col, k))
            source = (col - k + n_col) % n_col
            update = lax.dynamic_update_slice(
                update,
                piece.reshape(rows, part_width),
                (0, source * width + chunk * part_width),
            )
    return (update, new_momentum)


def solution(mesh):
    return jax.shard_map(
        shards,
        mesh=mesh,
        in_specs=(P(("row", "col"), None), P(("row", "col"), None)),
        out_specs=(P(("row", "col"), None), P(("row", "col"), None)),
        check_vma=False,
    )
```

time: 1110 us -> 802 us (0.72)
  waiting for transfers between devices: 740 us -> 384 us
  blocking collectives: 210 us -> 0 us
  starting transfers between devices: 0.39 us -> 128 us
  matrix products: 115 us -> 194 us
  local copies, waits for them, and re-layouts: 6.49 us -> 38.3 us
  other arithmetic: 19.1 us -> 48.8 us
    all_gather x3 -> x0, waiting for transfers between devices: 500 us -> none  [the longest x1 222 us: shards(): gram_panel = lax.all_gather(joined, 'col', axis=0, tiled=True)]
    ppermute x0 -> x88, waiting for transfers between devices: none -> 347 us  [the longest x30 161 us: next_in_ring(): return lax.ppermute(value, 'col', shift_pairs(n_col, 2))]
    reduce_scatter x2 -> x0, waiting for transfers between devices: 240 us -> none  [shards(): lax.psum_scatter(gram_term_rows(jnp.int32(0), share_rows * lax.axis_size(...]
    all_to_all x2 -> x0, blocking collectives: 170 us -> none  [the longest x1 84.9 us: shards(): lax.all_to_all(update_block, 'col', split_axis=0, concat_axis=1, tiled=True)]
    ppermute x0 -> x88, starting transfers between devices: none -> 114 us  [the longest x13 30.2 us: other_core(): return lax.ppermute(value, 'col', xor_pairs(n_col, 1))]
    dot_general x4 -> x41, matrix products: 115 us -> 194 us  [the longest x12 55.9 us: times_gram(): lax.dot_general(far[d], theirs[d][::-1], turned, preferred_element_type=F32)]
    psum x1 -> x0, blocking collectives: 40.1 us -> none  [shards(): sumsq = lax.psum(jnp.sum(direction * direction), ('row', 'col'))]
    all_to_all x0 -> x2, waiting for transfers between devices: none -> 37 us  [shards(): lax.all_to_all(raw[h * half:(h + 1) * half], 'col', split_axis=1, concat_...]
  transfers between devices with their start and end apart: 5 -> 90, of which waited for: 5 -> 44; matrix products, arithmetic and copies ran while one was open for 2% -> 27% of each run, Pallas kernels for 0% -> 0%
where the time goes in v1:
time: 802 us; the launch traced here: 798 us
  waiting for transfers between devices  384 us (48%)
  matrix products  194 us (24%)
  starting transfers between devices  128 us (16%)
  other arithmetic  48.8 us (6%)
  local copies, waits for them, and re-layouts  38.3 us (5%)
    ppermute x30, waiting for transfers between devices, next_in_ring(): return lax.ppermute(value, 'col', shift_pairs(n_col, 2))  161 us
    ppermute x28, waiting for transfers between devices, across(): return lax.ppermute(value, 'row', xor_pairs(n_row, distance))  111 us
    ppermute x14, waiting for transfers between devices, shards(): piece = lax.ppermute(piece, 'col', shift_pairs(n_col, k))  60.3 us
    dot_general x12, matrix products, times_gram(): lax.dot_general(far[d], theirs[d][::-1], turned, preferred_element_type=F32)  55.9 us
    dot_general x12, matrix products, times_gram(): lax.dot_general(near[d], theirs[d], plain, preferred_element_type=F32)  45.3 us
    dot_general x4, matrix products, times_gram(): total = lax.dot_general(corner, mine, plain, preferred_element_type=F32)  42.1 us
    all_to_all x2, waiting for transfers between devices, shards(): lax.all_to_all(raw[h * half:(h + 1) * half], 'col', split_axis=1, concat_...  37 us
    ppermute x13, starting transfers between devices, other_core(): return lax.ppermute(value, 'col', xor_pairs(n_col, 1))  30.2 us
  transfers between devices with their start and end apart: 90, of which 44 were waited for; matrix products, arithmetic and copies ran while one was open for 27% of the time, Pallas kernels for 0%

profile of v1, /device:TPU:9, one launch (start us, length us, event | category | flops | bytes accessed | tf_op | source)
XLA Modules:
  0.0 798.3 jit_solution(18402883266830658964)
XLA Ops:
  0.6 11.6 %fusion.39 = (bf16[224,8192]{1,0:T(8,128)(2,1)}, f32[224,8192]{1,0:T(8,128)}) fusion(f32[224,8192]{1,0:T(8,128)} %param.2, f32[224,8192]{1,0:T(8,128)} %param.3), kind=kLoop, calls=%fused_computation.75 | loop fusion | flops 9175040 | bytes 25690112 | tf_op jit(solution)/shard_map/convert_element_type | solution.py:52
  25.9 37.0 %all-to-all-done = bf16[112,8,1024]{2,0,1:T(8,128)(2,1)S(1)} async-done(((bf16[112,8,1024]{2,0,1:T(8,128)(2,1)}), bf16[112,8,1024]{2,0,1:T(8,128)(2,1)S(1)}, u32[]{:S(2)}, u32[]{:S(2)}) %all-to-all-start) | async-done | bytes 1835040 | tf_op jit(solution)/shard_map/all_to_all | solution.py:68
  88.0 13.5 %collective-permute-done.1 = f32[1,1]{1,0:T(1,128)} collective-permute-done((f32[1,1]{1,0:T(1,128)}, f32[1,1]{1,0:T(1,128)}, u32[]{:S(2)}, u32[]{:S(2)}) %collective-permute-start.1) | collective-permute-done | bytes 36 | tf_op jit(solution)/shard_map/ppermute | solution.py:57
  102.2 8.3 %collective-permute-start.2 = (f32[1,1]{1,0:T(1,128)}, f32[1,1]{1,0:T(1,128)}, u32[]{:S(2)}, u32[]{:S(2)}) collective-permute-start(f32[1,1]{1,0:T(1,128)} %add.740), channel_id=1, source_target_pairs={{0,4},{1,5},{2,6},{3,7},{4,0},{5,1},{6,2},{7,3},{8,12},{9,13},{10,... | collective-permute-start | bytes 20 | tf_op jit(solution)/shard_map/ppermute | solution.py:57
  179.9 37.3 %collective-permute-done.21 = bf16[896,1024]{1,0:T(8,128)(2,1)} collective-permute-done((bf16[896,1024]{1,0:T(8,128)(2,1)}, bf16[896,1024]{1,0:T(8,128)(2,1)}, u32[]{:S(2)}, u32[]{:S(2)}) %collective-permute-start.21) | collective-permute-done | bytes 1835040 | tf_op jit(solution)/shard_map/ppermute | solution.py:42
  228.9 12.0 %collective-permute-done.37 = bf16[896,1024]{1,0:T(8,128)(2,1)} collective-permute-done((bf16[896,1024]{1,0:T(8,128)(2,1)S(1)}, bf16[896,1024]{1,0:T(8,128)(2,1)}, u32[]{:S(2)}, u32[]{:S(2)}) %collective-permute-start.37) | collective-permute-done | bytes 1835040 | tf_op jit(solution)/shard_map/ppermute | solution.py:42
  272.7 12.5 %collective-permute-start.9 = (bf16[2,112,896]{2,1,0:T(8,128)(2,1)S(1)}, bf16[2,112,896]{2,1,0:T(8,128)(2,1)S(1)}, u32[]{:S(2)}, u32[]{:S(2)}) collective-permute-start(bf16[2,112,896]{2,1,0:T(8,128)(2,1)S(1)} %get-tuple-element.3), channel_id=1, source_target_pairs={{0,2},{1,3},{2,4},{3,5},{4,6},{5,7},{6,0},{7,1},{8,10},{9,11},{10,... | collective-permute-start | bytes 1204232 | tf_op jit(solution)/shard_map/ppermute | solution.py:48
  305.7 8.3 %collective-permute-done.24 = bf16[2,112,896]{2,1,0:T(8,128)(2,1)S(1)} collective-permute-done((bf16[2,112,896]{2,1,0:T(8,128)(2,1)S(1)}, bf16[2,112,896]{2,1,0:T(8,128)(2,1)S(1)}, u32[]{:S(2)}, u32[]{:S(2)}) %collective-permute-start.24) | collective-permute-done | bytes 401440 | tf_op jit(solution)/shard_map/ppermute | solution.py:48
  322.8 17.0 %collective-permute-done.25 = bf16[2,112,896]{2,1,0:T(8,128)(2,1)S(1)} collective-permute-done((bf16[2,112,896]{2,1,0:T(8,128)(2,1)S(1)}, bf16[2,112,896]{2,1,0:T(8,128)(2,1)S(1)}, u32[]{:S(2)}, u32[]{:S(2)}) %collective-permute-start.25) | collective-permute-done | bytes 401440 | tf_op jit(solution)/shard_map/ppermute | solution.py:48
  408.1 8.4 %collective-permute-done.29 = bf16[2,112,896]{2,1,0:T(8,128)(2,1)S(1)} collective-permute-done((bf16[2,112,896]{2,1,0:T(8,128)(2,1)S(1)}, bf16[2,112,896]{2,1,0:T(8,128)(2,1)S(1)}, u32[]{:S(2)}, u32[]{:S(2)}) %collective-permute-start.29) | collective-permute-done | bytes 401440 | tf_op jit(solution)/shard_map/ppermute | solution.py:48
  416.6 8.5 %collective-permute-done.55 = bf16[2,112,896]{2,1,0:T(8,128)(2,1)S(1)} collective-permute-done((bf16[2,112,896]{2,1,0:T(8,128)(2,1)S(1)}, bf16[2,112,896]{2,1,0:T(8,128)(2,1)S(1)}, u32[]{:S(2)}, u32[]{:S(2)}) %collective-permute-start.55) | collective-permute-done | bytes 401440 | tf_op jit(solution)/shard_map/ppermute | solution.py:48
  433.7 11.6 %collective-permute-start.30 = (bf16[4,2,112,896]{3,2,1,0:T(8,128)(2,1)S(1)}, bf16[4,2,112,896]{3,2,1,0:T(8,128)(2,1)S(1)}, u32[]{:S(2)}, u32[]{:S(2)}) collective-permute-start(bf16[4,2,112,896]{3,2,1,0:T(8,128)(2,1)S(1)} %pad_maximum_fusion.20), channel_id=1, source_target_pairs={{0,1},{1,0},{2,3},{3,2},{4,5},{5,4},{6,7},{7,6},{8,9},{9,8},{10,11... | collective-permute-start | bytes 4816904 | tf_op jit(solution)/shard_map/ppermute | solution.py:45
  449.1 9.5 %collective-permute-done.34 = bf16[2,112,896]{2,1,0:T(8,128)(2,1)S(1)} collective-permute-done((bf16[2,112,896]{2,1,0:T(8,128)(2,1)S(1)}, bf16[2,112,896]{2,1,0:T(8,128)(2,1)S(1)}, u32[]{:S(2)}, u32[]{:S(2)}) %collective-permute-start.34) | collective-permute-done | bytes 401440 | tf_op jit(solution)/shard_map/ppermute | solution.py:42
  461.6 13.3 %collective-permute-done.49 = bf16[2,112,896]{2,1,0:T(8,128)(2,1)S(1)} collective-permute-done((bf16[2,112,896]{2,1,0:T(8,128)(2,1)S(1)}, bf16[2,112,896]{2,1,0:T(8,128)(2,1)S(1)}, u32[]{:S(2)}, u32[]{:S(2)}) %collective-permute-start.49) | collective-permute-done | bytes 401440 | tf_op jit(solution)/shard_map/ppermute | solution.py:42
  478.3 11.8 %collective-permute-done.58 = bf16[2,112,896]{2,1,0:T(8,128)(2,1)S(1)} collective-permute-done((bf16[2,112,896]{2,1,0:T(8,128)(2,1)S(1)}, bf16[2,112,896]{2,1,0:T(8,128)(2,1)S(1)}, u32[]{:S(2)}, u32[]{:S(2)}) %collective-permute-start.58) | collective-permute-done | bytes 401440 | tf_op jit(solution)/shard_map/ppermute | solution.py:48
  558.9 9.1 %fusion.156 = (bf16[2,896,512]{2,1,0:T(8,128)(2,1)S(1)}, f32[2,896,512]{2,1,0:T(8,128)S(1)}) fusion(f32[2,896,512]{2,1,0:T(8,128)} %fusion.141, f32[2,896,512]{2,1,0:T(8,128)} %fusion.143, f32[2,896,512]{2,1,0:T(8,128)} %fusion.133, f32[2,896,512]{2,1,0:T(8,128)} %fusion.135, f32[2,896,512]{2,1,0:T(8,128)} %fusion.125, f32[2,896,512]{2,1,0:T(8,128)S(1)} %fusion.127, ...), kind=kOutput, calls=%fused_computation.373 | convolution fusion | flops 1653342208 | bytes 38076416 | tf_op jit(solution)/shard_map/dot_general | solution.py:146
  576.3 11.8 %fusion.155 = (bf16[2,896,512]{2,1,0:T(8,128)(2,1)}, f32[2,896,512]{2,1,0:T(8,128)S(1)}) fusion(f32[2,896,512]{2,1,0:T(8,128)} %fusion.145, f32[2,896,512]{2,1,0:T(8,128)} %fusion.147, f32[2,896,512]{2,1,0:T(8,128)} %fusion.137, f32[2,896,512]{2,1,0:T(8,128)} %fusion.139, f32[2,896,512]{2,1,0:T(8,128)} %fusion.129, f32[2,896,512]{2,1,0:T(8,128)} %fusion.131, ...), kind=kOutput, calls=%fused_computation.372 | convolution fusion | flops 1653342208 | bytes 38076416 | tf_op jit(solution)/shard_map/dot_general | solution.py:146
  600.7 8.6 %collective-permute-done.77 = bf16[2,896,512]{2,1,0:T(8,128)(2,1)} collective-permute-done((bf16[2,896,512]{2,1,0:T(8,128)(2,1)S(1)}, bf16[2,896,512]{2,1,0:T(8,128)(2,1)}, u32[]{:S(2)}, u32[]{:S(2)}) %collective-permute-start.77) | collective-permute-done | bytes 1835040 | tf_op jit(solution)/shard_map/ppermute | solution.py:42
  622.7 25.8 %collective-permute-done.66 = bf16[2,896,512]{2,1,0:T(8,128)(2,1)S(1)} collective-permute-done((bf16[2,896,512]{2,1,0:T(8,128)(2,1)}, bf16[2,896,512]{2,1,0:T(8,128)(2,1)S(1)}, u32[]{:S(2)}, u32[]{:S(2)}) %collective-permute-start.66) | collective-permute-done | bytes 1835040 | tf_op jit(solution)/shard_map/ppermute | solution.py:42
  697.5 10.8 %fusion.18 = bf16[2,896,512]{2,1,0:T(8,128)(2,1)S(1)} fusion(f32[2,896,512]{2,1,0:T(8,128)} %fusion.55, f32[2,896,512]{2,1,0:T(8,128)} %fusion.56, f32[2,896,512]{2,1,0:T(8,128)} %fusion.57, f32[2,896,512]{2,1,0:T(8,128)} %fusion.58, f32[2,896,512]{2,1,0:T(8,128)} %fusion.59, f32[2,896,512]{2,1,0:T(8,128)} %fusion.60, ...), kind=kOutput, calls=%fused_computation.47 | convolution fusion | flops 1659764736 | bytes 39911428 | tf_op jit(solution)/shard_map/dot_general | solution.py:146
  718.4 10.5 %fusion.34 = bf16[2,896,512]{2,1,0:T(8,128)(2,1)S(1)} fusion(f32[2,896,512]{2,1,0:T(8,128)} %fusion.49, f32[2,896,512]{2,1,0:T(8,128)} %fusion.50, f32[2,896,512]{2,1,0:T(8,128)} %fusion.51, f32[2,896,512]{2,1,0:T(8,128)} %fusion.52, f32[2,896,512]{2,1,0:T(8,128)} %fusion.53, f32[2,896,512]{2,1,0:T(8,128)} %fusion.54, ...), kind=kOutput, calls=%fused_computation.65 | convolution fusion | flops 1659764736 | bytes 39911428 | tf_op jit(solution)/shard_map/dot_general | solution.py:146
  732.7 14.6 %collective-permute-done.72 = bf16[2,112,512]{2,1,0:T(8,128)(2,1)S(1)} collective-permute-done((bf16[2,112,512]{2,1,0:T(8,128)(2,1)}, bf16[2,112,512]{2,1,0:T(8,128)(2,1)S(1)}, u32[]{:S(2)}, u32[]{:S(2)}) %collective-permute-start.72) | collective-permute-done | bytes 229408 | tf_op jit(solution)/shard_map/ppermute | solution.py:180
  752.3 19.1 %collective-permute-done.75 = bf16[2,112,512]{2,1,0:T(8,128)(2,1)S(1)} collective-permute-done((bf16[2,112,512]{2,1,0:T(8,128)(2,1)S(1)}, bf16[2,112,512]{2,1,0:T(8,128)(2,1)S(1)}, u32[]{:S(2)}, u32[]{:S(2)}) %collective-permute-start.75) | collective-permute-done | bytes 229408 | tf_op jit(solution)/shard_map/ppermute | solution.py:180
  774.6 17.1 %collective-permute-done.84 = bf16[2,112,512]{2,1,0:T(8,128)(2,1)S(1)} collective-permute-done((bf16[2,112,512]{2,1,0:T(8,128)(2,1)S(1)}, bf16[2,112,512]{2,1,0:T(8,128)(2,1)S(1)}, u32[]{:S(2)}, u32[]{:S(2)}) %collective-permute-start.84) | collective-permute-done | bytes 229408 | tf_op jit(solution)/shard_map/ppermute | solution.py:180
  (423 shorter events, 444.2 us)
Async XLA Ops:
  17.3 45.5 %all-to-all-start = ((bf16[112,8,1024]{2,0,1:T(8,128)(2,1)}), bf16[112,8,1024]{2,0,1:T(8,128)(2,1)S(1)}, u32[]{:S(2)}, u32[]{:S(2)}) async-start(bf16[112,8,1024]{2,0,1:T(8,128)(2,1)} %bitcast.635), calls=%async_computation | async-start | bytes 3670016 | tf_op jit(solution)/shard_map/all_to_all | solution.py:68
  62.8 54.5 %all-to-all-start.1 = ((bf16[112,8,1024]{2,0,1:T(8,128)(2,1)}), bf16[112,8,1024]{2,0,1:T(8,128)(2,1)}, u32[]{:S(2)}, u32[]{:S(2)}) async-start(bf16[112,8,1024]{2,0,1:T(8,128)(2,1)} %bitcast.634), calls=%async_computation.1 | async-start | bytes 3670016 | tf_op jit(solution)/shard_map/all_to_all | solution.py:68
  137.6 79.6 %collective-permute-start.21 = (bf16[896,1024]{1,0:T(8,128)(2,1)}, bf16[896,1024]{1,0:T(8,128)(2,1)}, u32[]{:S(2)}, u32[]{:S(2)}) collective-permute-start(bf16[896,1024]{1,0:T(8,128)(2,1)} %bitcast.34), channel_id=1, source_target_pairs={{0,8},{8,0},{16,24},{24,16},{1,9},{9,1},{17,25},{25,17},{2,10},{10... | collective-permute-start | bytes 5505032 | tf_op jit(solution)/shard_map/ppermute | solution.py:42
  162.1 66.9 %collective-permute-start.36 = (bf16[896,1024]{1,0:T(8,128)(2,1)}, bf16[896,1024]{1,0:T(8,128)(2,1)}, u32[]{:S(2)}, u32[]{:S(2)}) collective-permute-start(bf16[896,1024]{1,0:T(8,128)(2,1)} %bitcast.34), channel_id=1, source_target_pairs={{0,16},{8,24},{16,0},{24,8},{1,17},{9,25},{17,1},{25,9},{2,18},{10... | collective-permute-start | bytes 5505032 | tf_op jit(solution)/shard_map/ppermute | solution.py:42
  169.0 72.0 %collective-permute-start.37 = (bf16[896,1024]{1,0:T(8,128)(2,1)S(1)}, bf16[896,1024]{1,0:T(8,128)(2,1)}, u32[]{:S(2)}, u32[]{:S(2)}) collective-permute-start(bf16[896,1024]{1,0:T(8,128)(2,1)S(1)} %bitcast.622), channel_id=1, source_target_pairs={{0,16},{8,24},{16,0},{24,8},{1,17},{9,25},{17,1},{25,9},{2,18},{10... | collective-permute-start | bytes 5505032 | tf_op jit(solution)/shard_map/ppermute | solution.py:42
  176.8 69.9 %collective-permute-start.6 = (bf16[2,112,896]{2,1,0:T(8,128)(2,1)S(1)}, bf16[2,112,896]{2,1,0:T(8,128)(2,1)S(1)}, u32[]{:S(2)}, u32[]{:S(2)}) collective-permute-start(bf16[2,112,896]{2,1,0:T(8,128)(2,1)S(1)} %dynamic-slice_bitcast_fusion.4), channel_id=1, source_target_pairs={{0,2},{1,3},{2,4},{3,5},{4,6},{5,7},{6,0},{7,1},{8,10},{9,11},{10,... | collective-permute-start | bytes 1204232 | tf_op jit(solution)/shard_map/ppermute | solution.py:48
  177.9 65.4 %collective-permute-start.19 = (bf16[1,112,896]{2,1,0:T(8,128)(2,1)S(1)}, bf16[1,112,896]{2,1,0:T(8,128)(2,1)S(1)}, u32[]{:S(2)}, u32[]{:S(2)}) collective-permute-start(bf16[1,112,896]{2,1,0:T(8,128)(2,1)S(1)} %collective-permute-done.18), channel_id=1, source_target_pairs={{0,2},{1,3},{2,4},{3,5},{4,6},{5,7},{6,0},{7,1},{8,10},{9,11},{10,... | collective-permute-start | bytes 602120 | tf_op jit(solution)/shard_map/ppermute | solution.py:48
  227.9 67.8 %collective-permute-start.23 = (bf16[2,4,112,896]{3,2,0,1:T(8,128)(2,1)}, bf16[2,4,112,896]{3,2,0,1:T(8,128)(2,1)S(1)}, u32[]{:S(2)}, u32[]{:S(2)}) collective-permute-start(bf16[2,4,112,896]{3,2,0,1:T(8,128)(2,1)} %bitcast.613), channel_id=1, source_target_pairs={{0,1},{1,0},{2,3},{3,2},{4,5},{5,4},{6,7},{7,6},{8,9},{9,8},{10,11... | collective-permute-start | bytes 4816904 | tf_op jit(solution)/shard_map/ppermute | solution.py:45
  254.2 43.4 %collective-permute-start.38 = (bf16[2,4,112,896]{3,2,0,1:T(8,128)(2,1)S(1)}, bf16[2,4,112,896]{3,2,0,1:T(8,128)(2,1)S(1)}, u32[]{:S(2)}, u32[]{:S(2)}) collective-permute-start(bf16[2,4,112,896]{3,2,0,1:T(8,128)(2,1)S(1)} %bitcast.695), channel_id=1, source_target_pairs={{0,1},{1,0},{2,3},{3,2},{4,5},{5,4},{6,7},{7,6},{8,9},{9,8},{10,11... | collective-permute-start | bytes 4816904 | tf_op jit(solution)/shard_map/ppermute | solution.py:45
  254.5 50.8 %collective-permute-start.51 = (bf16[896,1024]{1,0:T(8,128)(2,1)}, bf16[896,1024]{1,0:T(8,128)(2,1)S(1)}, u32[]{:S(2)}, u32[]{:S(2)}) collective-permute-start(bf16[896,1024]{1,0:T(8,128)(2,1)} %collective-permute-done.36), channel_id=1, source_target_pairs={{0,8},{8,0},{16,24},{24,16},{1,9},{9,1},{17,25},{25,17},{2,10},{10... | collective-permute-start | bytes 5505032 | tf_op jit(solution)/shard_map/ppermute | solution.py:42
  259.3 46.1 %collective-permute-start.52 = (bf16[896,1024]{1,0:T(8,128)(2,1)}, bf16[896,1024]{1,0:T(8,128)(2,1)S(1)}, u32[]{:S(2)}, u32[]{:S(2)}) collective-permute-start(bf16[896,1024]{1,0:T(8,128)(2,1)} %collective-permute-done.22), channel_id=1, source_target_pairs={{0,16},{8,24},{16,0},{24,8},{1,17},{9,25},{17,1},{25,9},{2,18},{10... | collective-permute-start | bytes 5505032 | tf_op jit(solution)/shard_map/ppermute | solution.py:42
  340.4 44.7 %collective-permute-start.53 = (bf16[2,4,112,896]{3,2,0,1:T(8,128)(2,1)S(1)}, bf16[2,4,112,896]{3,2,0,1:T(8,128)(2,1)S(1)}, u32[]{:S(2)}, u32[]{:S(2)}) collective-permute-start(bf16[2,4,112,896]{3,2,0,1:T(8,128)(2,1)S(1)} %bitcast.694), channel_id=1, source_target_pairs={{0,1},{1,0},{2,3},{3,2},{4,5},{5,4},{6,7},{7,6},{8,9},{9,8},{10,11... | collective-permute-start | bytes 4816904 | tf_op jit(solution)/shard_map/ppermute | solution.py:45
  347.4 51.9 %collective-permute-start.12 = (bf16[4,2,112,896]{3,2,1,0:T(8,128)(2,1)S(1)}, bf16[4,2,112,896]{3,2,1,0:T(8,128)(2,1)S(1)}, u32[]{:S(2)}, u32[]{:S(2)}) collective-permute-start(bf16[4,2,112,896]{3,2,1,0:T(8,128)(2,1)S(1)} %pad_maximum_fusion.19), channel_id=1, source_target_pairs={{0,1},{1,0},{2,3},{3,2},{4,5},{5,4},{6,7},{7,6},{8,9},{9,8},{10,11... | collective-permute-start | bytes 4816904 | tf_op jit(solution)/shard_map/ppermute | solution.py:45
  382.8 64.0 %collective-permute-start.32 = (bf16[2,112,896]{2,1,0:T(8,128)(2,1)S(1)}, bf16[2,112,896]{2,1,0:T(8,128)(2,1)S(1)}, u32[]{:S(2)}, u32[]{:S(2)}) collective-permute-start(bf16[2,112,896]{2,1,0:T(8,128)(2,1)S(1)} %reverse_select_fusion.10), channel_id=1, source_target_pairs={{0,8},{8,0},{16,24},{24,16},{1,9},{9,1},{17,25},{25,17},{2,10},{10... | collective-permute-start | bytes 1204232 | tf_op jit(solution)/shard_map/ppermute | solution.py:42
  384.1 63.9 %collective-permute-start.47 = (bf16[2,112,896]{2,1,0:T(8,128)(2,1)S(1)}, bf16[2,112,896]{2,1,0:T(8,128)(2,1)S(1)}, u32[]{:S(2)}, u32[]{:S(2)}) collective-permute-start(bf16[2,112,896]{2,1,0:T(8,128)(2,1)S(1)} %reverse_select_fusion.6), channel_id=1, source_target_pairs={{0,16},{8,24},{16,0},{24,8},{1,17},{9,25},{17,1},{25,9},{2,18},{10... | collective-permute-start | bytes 1204232 | tf_op jit(solution)/shard_map/ppermute | solution.py:42
  399.3 49.7 %collective-permute-start.33 = (bf16[2,112,896]{2,1,0:T(8,128)(2,1)S(1)}, bf16[2,112,896]{2,1,0:T(8,128)(2,1)S(1)}, u32[]{:S(2)}, u32[]{:S(2)}) collective-permute-start(bf16[2,112,896]{2,1,0:T(8,128)(2,1)S(1)} %reverse_select_fusion.9), channel_id=1, source_target_pairs={{0,8},{8,0},{16,24},{24,16},{1,9},{9,1},{17,25},{25,17},{2,10},{10... | collective-permute-start | bytes 1204232 | tf_op jit(solution)/shard_map/ppermute | solution.py:42
  433.7 58.4 %collective-permute-start.30 = (bf16[4,2,112,896]{3,2,1,0:T(8,128)(2,1)S(1)}, bf16[4,2,112,896]{3,2,1,0:T(8,128)(2,1)S(1)}, u32[]{:S(2)}, u32[]{:S(2)}) collective-permute-start(bf16[4,2,112,896]{3,2,1,0:T(8,128)(2,1)S(1)} %pad_maximum_fusion.20), channel_id=1, source_target_pairs={{0,1},{1,0},{2,3},{3,2},{4,5},{5,4},{6,7},{7,6},{8,9},{9,8},{10,11... | collective-permute-start | bytes 4816904 | tf_op jit(solution)/shard_map/ppermute | solution.py:45
  477.9 51.9 %collective-permute-start.50 = (bf16[4,2,112,896]{3,2,1,0:T(8,128)(2,1)}, bf16[4,2,112,896]{3,2,1,0:T(8,128)(2,1)}, u32[]{:S(2)}, u32[]{:S(2)}) collective-permute-start(bf16[4,2,112,896]{3,2,1,0:T(8,128)(2,1)} %pad_maximum_fusion.23), channel_id=1, source_target_pairs={{0,1},{1,0},{2,3},{3,2},{4,5},{5,4},{6,7},{7,6},{8,9},{9,8},{10,11... | collective-permute-start | bytes 4816904 | tf_op jit(solution)/shard_map/ppermute | solution.py:45
  490.0 53.2 %collective-permute-start.62 = (bf16[2,112,896]{2,1,0:T(8,128)(2,1)}, bf16[2,112,896]{2,1,0:T(8,128)(2,1)S(1)}, u32[]{:S(2)}, u32[]{:S(2)}) collective-permute-start(bf16[2,112,896]{2,1,0:T(8,128)(2,1)} %reverse_select_fusion.2), channel_id=1, source_target_pairs={{0,24},{8,16},{16,8},{24,0},{1,25},{9,17},{17,9},{25,1},{2,26},{10... | collective-permute-start | bytes 1204232 | tf_op jit(solution)/shard_map/ppermute | solution.py:42
  492.1 51.2 %collective-permute-start.63 = (bf16[2,112,896]{2,1,0:T(8,128)(2,1)}, bf16[2,112,896]{2,1,0:T(8,128)(2,1)S(1)}, u32[]{:S(2)}, u32[]{:S(2)}) collective-permute-start(bf16[2,112,896]{2,1,0:T(8,128)(2,1)} %reverse_select_fusion.1), channel_id=1, source_target_pairs={{0,24},{8,16},{16,8},{24,0},{1,25},{9,17},{17,9},{25,1},{2,26},{10... | collective-permute-start | bytes 1204232 | tf_op jit(solution)/shard_map/ppermute | solution.py:42
  588.1 60.4 %collective-permute-start.66 = (bf16[2,896,512]{2,1,0:T(8,128)(2,1)}, bf16[2,896,512]{2,1,0:T(8,128)(2,1)S(1)}, u32[]{:S(2)}, u32[]{:S(2)}) collective-permute-start(bf16[2,896,512]{2,1,0:T(8,128)(2,1)} %get-tuple-element.62), channel_id=1, source_target_pairs={{0,8},{8,0},{16,24},{24,16},{1,9},{9,1},{17,25},{25,17},{2,10},{10... | collective-permute-start | bytes 5505032 | tf_op jit(solution)/shard_map/ppermute | solution.py:42
  599.5 66.5 %collective-permute-start.67 = (bf16[2,896,512]{2,1,0:T(8,128)(2,1)S(1)}, bf16[2,896,512]{2,1,0:T(8,128)(2,1)S(1)}, u32[]{:S(2)}, u32[]{:S(2)}) collective-permute-start(bf16[2,896,512]{2,1,0:T(8,128)(2,1)S(1)} %copy-done.2), channel_id=1, source_target_pairs={{0,16},{8,24},{16,0},{24,8},{1,17},{9,25},{17,1},{25,9},{2,18},{10... | collective-permute-start | bytes 5505032 | tf_op jit(solution)/shard_map/ppermute | solution.py:42
  610.9 64.8 %collective-permute-start.80 = (bf16[896,512]{1,0:T(8,128)(2,1)S(1)}, bf16[896,512]{1,0:T(8,128)(2,1)}, u32[]{:S(2)}, u32[]{:S(2)}) collective-permute-start(bf16[896,512]{1,0:T(8,128)(2,1)S(1)} %get-tuple-element.39), channel_id=1, source_target_pairs={{0,16},{8,24},{16,0},{24,8},{1,17},{9,25},{17,1},{25,9},{2,18},{10... | collective-permute-start | bytes 2752520 | tf_op jit(solution)/shard_map/ppermute | solution.py:42
  613.2 62.5 %collective-permute-start.79 = (bf16[896,512]{1,0:T(8,128)(2,1)S(1)}, bf16[896,512]{1,0:T(8,128)(2,1)S(1)}, u32[]{:S(2)}, u32[]{:S(2)}) collective-permute-start(bf16[896,512]{1,0:T(8,128)(2,1)S(1)} %get-tuple-element.42), channel_id=1, source_target_pairs={{0,8},{8,0},{16,24},{24,16},{1,9},{9,1},{17,25},{25,17},{2,10},{10... | collective-permute-start | bytes 2752520 | tf_op jit(solution)/shard_map/ppermute | solution.py:42
  (102 other events, 1661.2 us)

commit v2 on v0

v2 whole, which is shorter than its diff:
```python
import math

import functools

import jax
import jax.numpy as jnp
from jax import lax
from jax.experimental import pallas as pl
from jax.experimental.pallas import tpu as pltpu
from jax.sharding import PartitionSpec as P

momentum_coef = 0.95
rms_target = 0.4
coef_a = 3.4445
coef_b = -4.775
coef_c = 2.0315
TILE = 256
VMEM = 56 * 1024 * 1024
F32 = jnp.float32
BF16 = jnp.bfloat16


def xor_pairs(size, distance):
    return [(i, i ^ distance) for i in range(size)]


def shift_pairs(size, distance):
    return [(i, (i + distance) % size) for i in range(size)]


def low_bit(distance):
    return (distance & -distance).bit_length() - 1


class Slots:
    def __init__(self):
        self.ended, self.noted = None, []

    def hold(self, value):
        return value if self.ended is None else lax.optimization_barrier((value, self.ended))[0]

    def note(self, value):
        self.noted.append(value)
        return value

    def close(self):
        if self.noted:
            self.ended = lax.optimization_barrier(tuple(self.noted))[0]
            self.noted = []


def direction_kernel(grad, momentum, new_momentum, upper, lower, sumsq, squares):
    lower_half, part = pl.program_id(0), pl.program_id(1)
    state = momentum_coef * momentum[...] + grad[...]
    new_momentum[...] = state
    direction = grad[...] + momentum_coef * state
    width = upper.shape[2]

    @pl.when((lower_half == 0) & (part == 0))
    def _():
        squares[...] = jnp.zeros_like(squares)

    for out, mine in ((upper, lower_half == 0), (lower, lower_half == 1)):

        @pl.when(mine)
        def _(out=out):
            for group in range(out.shape[0]):
                out[group] = direction[:, group * width : (group + 1) * width].astype(BF16)

    total = squares[...]
    for row in range(0, direction.shape[0], 8):
        rows = direction[row : row + 8]
        total = total + rows * rows
    squares[...] = total

    @pl.when((lower_half == 1) & (part == pl.num_programs(1) - 1))
    def _():
        sumsq[0, 0] = jnp.sum(squares[...])


def direction_step(grad, momentum, n_col):
    rows, n_in = grad.shape
    half, width = rows // 2, n_in // n_col
    if half % 16:
        state = momentum_coef * momentum + grad
        direction = grad + momentum_coef * state
        raw = direction.astype(BF16).reshape(2, half, n_col, width).transpose(0, 2, 1, 3)
        return state, raw[0], raw[1], jnp.sum(direction * direction).reshape(1, 1)
    parts = 2
    tile = pl.BlockSpec((half, n_in // parts), lambda i, j: (i, j))
    groups = (n_col // parts, half, width)
    return pl.pallas_call(
        direction_kernel,
        grid=(2, parts),
        in_specs=[tile, tile],
        out_specs=[
            tile,
            pl.BlockSpec(groups, lambda i, j: (jnp.where(i == 0, j, parts - 1), 0, 0)),
            pl.BlockSpec(groups, lambda i, j: (jnp.where(i == 0, 0, j), 0, 0)),
            pl.BlockSpec(memory_space=pltpu.SMEM),
        ],
        out_shape=[
            jax.ShapeDtypeStruct((rows, n_in), F32),
            jax.ShapeDtypeStruct((n_col, half, width), BF16),
            jax.ShapeDtypeStruct((n_col, half, width), BF16),
            jax.ShapeDtypeStruct((1, 1), F32),
        ],
        scratch_shapes=[pltpu.VMEM((8, n_in // parts), F32)],
        compiler_params=pltpu.CompilerParams(vmem_limit_bytes=VMEM),
    )(grad, momentum)


def absorb_kernel(n_ring, half, first_near, mirrored, seeded, scaled, *refs):
    places, refs = refs[0], refs[1:]
    if scaled:
        scale, refs = refs[0], refs[1:]
    near, refs = refs[: 2 * n_ring], refs[2 * n_ring :]
    if not mirrored:
        far, refs = refs[: 2 * n_ring], refs[2 * n_ring :]
    value, refs = refs[0], refs[1:]
    if seeded:
        before, refs = refs[0], refs[1:]
    block, total, refs = refs[0], refs[1], refs[2:]
    if scaled:
        rounded, refs = refs[0], refs[1:]
    turned, sems = refs
    tall = block.shape[0] // 2

    @pl.when(pl.program_id(0) == 0)
    def _():
        copies = []

        def place(source, target):
            copy = pltpu.make_async_copy(source, target, sems.at[len(copies)])
            copy.start()
            copies.append(copy)

        for k in range(2 * n_ring):
            at = pl.ds(pl.multiple_of(places[k], 16), half)
            below = pl.ds(pl.multiple_of(places[k] + tall, 16), half)
            place(near[k].at[first_near], block.at[at, pl.ds(0, tall)])
            place(near[k].at[first_near + 1], block.at[below, pl.ds(tall, tall)])
            if mirrored:
                place(near[k].at[first_near + 2], block.at[at, pl.ds(tall, tall)])
            else:
                place(far[k].at[0], turned.at[0, at])
                place(far[k].at[1], turned.at[1, at])
        for copy in copies:
            copy.wait()
        for j in range(0, tall, 128):
            if mirrored:
                block[pl.ds(tall + j, 128), pl.ds(0, tall)] = block[
                    pl.ds(0, tall), pl.ds(tall + j, 128)
                ].T
            else:
                block[pl.ds(j, 128), pl.ds(tall, tall)] = turned[0, :, pl.ds(j, 128)].T
                block[pl.ds(tall + j, 128), pl.ds(0, tall)] = turned[1, :, pl.ds(j, 128)].T

    result = jnp.dot(block[...], value[...], preferred_element_type=F32)
    if seeded:
        result = result + before[...]
    if scaled:
        result = result * scale[0]
        rounded[...] = result.astype(BF16)
    total[...] = result


def absorb(places, near, first_near, far, value, wide, before=None, scale=None):
    _, half, tall = near[0].shape
    tile = min(TILE, wide)
    whole = pl.BlockSpec(memory_space=pl.ANY)
    scalars = pl.BlockSpec(memory_space=pltpu.SMEM)
    column = pl.BlockSpec((2 * tall, tile), lambda n: (0, n))
    operands, specs = [places], [scalars]
    if scale is not None:
        operands.append(scale)
        specs.append(scalars)
    operands += [*near, *far, value]
    specs += [whole] * (len(near) + len(far)) + [column]
    if before is not None:
        operands.append(before)
        specs.append(column)
    shapes = [
        jax.ShapeDtypeStruct((2 * tall, 2 * tall), BF16),
        jax.ShapeDtypeStruct((2 * tall, wide), F32),
    ]
    out_specs = [pl.BlockSpec((2 * tall, 2 * tall), lambda n: (0, 0)), column]
    if scale is not None:
        shapes.append(jax.ShapeDtypeStruct((2 * tall, wide), BF16))
        out_specs.append(column)
    return pl.pallas_call(
        functools.partial(
            absorb_kernel,
            len(near) // 2,
            half,
            first_near,
            not far,
            before is not None,
            scale is not None,
        ),
        grid=(wide // tile,),
        in_specs=specs,
        out_specs=out_specs,
        out_shape=shapes,
        scratch_shapes=[
            pltpu.VMEM((2, tall, tall), BF16),
            pltpu.SemaphoreType.DMA((4 * len(near),)),
        ],
        compiler_params=pltpu.CompilerParams(vmem_limit_bytes=VMEM),
        cost_estimate=pl.CostEstimate(
            flops=8 * tall * tall * wide, bytes_accessed=30 * tall * tall, transcendentals=0
        ),
    )(*operands)


def shards(grad, momentum):
    n_row, n_col = lax.axis_size("row"), lax.axis_size("col")
    n_ring = n_col // 2
    row, col = lax.axis_index("row"), lax.axis_index("col")
    ring, core = col // 2, col % 2
    rows, n_in = grad.shape
    half = rows // 2
    width = n_in // n_col
    tall = half * n_col
    m_total = rows * n_row * n_col
    slots = Slots()

    def after(value, *others):
        return lax.optimization_barrier((value, *others))[0]

    def across(value, distance):
        return lax.ppermute(value, "row", xor_pairs(n_row, distance))

    def other_core(value):
        return lax.ppermute(value, "col", xor_pairs(n_col, 1))

    def next_in_ring(value):
        return lax.ppermute(value, "col", shift_pairs(n_col, 2))

    new_momentum, *raw_halves, sumsq = direction_step(grad, momentum, n_col)

    sumsq = sumsq + other_core(sumsq)
    step = 1
    while step < n_row:
        sumsq = sumsq + across(sumsq, step)
        step *= 2
    raw_halves[1] = after(raw_halves[1], sumsq)

    near = (1, 2) if n_row == 4 else tuple(range(1, n_row))
    own = []
    for h in range(2):
        block = lax.all_to_all(raw_halves[h], "col", split_axis=0, concat_axis=0)
        own.append(block.reshape(tall, width))
        if h == 0:
            others = [{d: across(own[0], d) for d in near}, {}]
    own[1] = after(own[1], *others[0].values())
    own2 = jnp.stack(own)
    cut = tall // 2

    def is_upper(d):
        return ((row >> low_bit(d)) & 1) == 1

    def swapped(first_half, second_half, d):
        return jnp.stack(
            [
                jnp.where(is_upper(d), second_half, first_half),
                jnp.where(is_upper(d), first_half, second_half),
            ]
        )

    own2 = jnp.stack(own)
    mixed = {}

    def gram_term(left, right):
        return lax.dot_general(
            left, right, (((2,), (2,)), ((0,), (0,))), preferred_element_type=F32
        ).astype(BF16)

    class Reduce:
        def __init__(self, terms):
            self.pieces = [term.reshape(-1, n_ring, 2, half, tall) for term in terms]
            self.parts = [self.part(t) for t in range(n_ring)]
            self.done = 0
            self.total = self.parts[0].astype(BF16)

        def part(self, t):
            index = (ring + n_ring - 1 - t) % n_ring
            sent, kept = self.pick(index, 1 - core), self.pick(index, core)
            return slots.note(kept.astype(F32) + other_core(sent).astype(F32))

        def pick(self, index, which):
            zero = jnp.zeros((), jnp.int32)
            picked = []
            for piece in self.pieces:
                sizes = (piece.shape[0], 1, 1, half, tall)
                part = lax.dynamic_slice(slots.hold(piece), (zero, index, which, zero, zero), sizes)
                picked.append(part.reshape(-1, half, tall))
            return picked[0] if len(picked) == 1 else jnp.concatenate(picked)

        def step(self):
            self.done += 1
            moved = slots.note(next_in_ring(slots.hold(self.total)))
            self.total = (moved.astype(F32) + self.parts[self.done]).astype(BF16)

    class Gather:
        def __init__(self, piece, distances):
            self.distances = distances
            self.found, self.partner = [piece], []
            self.crossed = {d: ([], []) for d in distances}
            self.left = list(enumerate(distances)) or [(0, 0)]

        @property
        def taken(self):
            return not self.left

        def complete(self):
            shared = [self.partner, *[theirs for _, theirs in self.crossed.values()]]
            return all(len(pieces) == n_ring for pieces in shared)

        def take_next(self, total, scale=None):
            i, d = self.left.pop(0)
            pieces = self.found + self.partner
            far = self.crossed[d][0] + self.crossed[d][1] if d else []
            value = flat(mixed[d] if d else own2)
            blocks[d], *made = take(pieces, 2 * i, far, value, total, None if self.left else scale)
            return made[0], made[1:]

        def step(self):
            self.found.append(slots.note(next_in_ring(slots.hold(self.found[-1]))))

        def share(self, held=True):
            hold = slots.hold if held else lambda value: value
            note = slots.note if held else lambda value: value
            for d in self.distances:
                mine, theirs = self.crossed[d]
                for part in mine[len(theirs) :]:
                    theirs.append(note(other_core(hold(part))))
            for piece in self.found[len(self.partner) :]:
                self.partner.append(note(other_core(hold(piece))))
                for i, d in enumerate(self.distances):
                    part = hold(piece[2 * i : 2 * i + 2])
                    part = jnp.where(is_upper(d), jnp.flip(part, 0), part)
                    self.crossed[d][0].append(note(across(part, d)))

    places = [(ring - k + n_ring) % n_ring for k in range(n_ring)]
    places = [(2 * place + core) * half for place in places] + [
        (2 * place + 1 - core) * half for place in places
    ]
    places = jnp.stack(places).astype(jnp.int32)
    n_in_line = 2 * tall
    wide = width // 2
    aligned = half % 16 == 0 and tall % 128 == 0

    def take(near, first_near, far, value, before=None, scale=None):
        if aligned:
            return absorb(places, near, first_near, far, value, wide, before, scale)

        def tiles(pieces):
            full = jnp.zeros((pieces[0].shape[0], tall, tall), BF16)
            for k, piece in enumerate(pieces):
                full = lax.dynamic_update_slice(full, piece, (0, places[k], 0))
            return full

        near = tiles([piece[first_near : first_near + (2 if far else 3)] for piece in near])
        b, c = tiles(far).transpose(0, 2, 1) if far else (near[2], near[2].T)
        block = jnp.concatenate(
            [jnp.concatenate([near[0], b], axis=1), jnp.concatenate([c, near[1]], axis=1)], axis=0
        )
        block = lax.optimization_barrier(block)
        total = jnp.dot(block, value[:, :wide], preferred_element_type=F32)
        total = total if before is None else total + before
        if scale is None:
            return block, total
        total = total * scale[0]
        return block, total, total.astype(BF16)

    def flat(value):
        return value.reshape(n_in_line, value.shape[-1])

    distances = list(range(1, n_row))
    groups = [distances[i : i + 2] for i in range(0, len(distances), 2)]
    blocks = {}
    moving = {}

    def move_second_half(part):
        for d in near:
            moving[d, part] = slots.note(across(slots.hold(own[1][part]), d))

    def move_to_diagonal(part):
        if n_row == 4:
            one, two = slots.hold(others[0][1][part]), slots.hold(moving[2, part])
            moving[3, 0, part] = slots.note(across(one, 2))
            moving[3, 1, part] = slots.note(across(two, 1))

    def make_term(d):
        if d in near:
            lower = jnp.concatenate([moving[d, part] for part in parts])
            upper = others[0][d]
        else:
            upper, lower = [jnp.concatenate([moving[3, h, part] for part in parts]) for h in range(2)]
        mixed[d] = swapped(slots.hold(upper), slots.hold(lower), d)
        return slots.note(gram_term(own2, mixed[d]))

    parts = (slice(0, cut), slice(cut, tall))
    move_second_half(parts[0])
    reduces = [[Reduce([gram_term(own2, own2), gram_term(own2[:1], own2[1:])]), []]]
    slots.close()
    gathers, terms = [], {}
    total, rounded = None, None
    waiting = [(d, 3 if d in near else 5) for d in distances]
    number = 2
    while reduces or waiting or terms or any(len(g.found) < n_ring for g in gathers):
        if number == 2:
            move_second_half(parts[1])
            step = 2
            sumsq = slots.hold(sumsq)
            while step < n_col:
                sumsq = sumsq + lax.ppermute(sumsq, "col", xor_pairs(n_col, step))
                step *= 2
            slots.note(sumsq)
        elif number in (3, 4):
            move_to_diagonal(parts[number - 3])
        for gather in gathers:
            gather.share()
        stepping = [run for run, _ in reduces][:2]
        stepping += [g for g in gathers if g.distances and len(g.found) < n_ring][: 2 - len(stepping)][:1]
        stepping += [g for g in gathers if not g.distances and len(g.found) < n_ring]
        for run in stepping:
            run.step()
        opened = None
        if groups and number >= 3:
            for group in groups[:1]:
                if all(d in terms for d in group):
                    opened = [Reduce([terms.pop(d) for d in group]), groups.pop(0)]
        if waiting and number >= waiting[0][1]:
            d = waiting.pop(0)[0]
            terms[d] = make_term(d)
        complete = [gather for gather in gathers if gather.complete() and not gather.taken]
        if complete and (groups or reduces or gathers[-1] is not complete[0]):
            total, rounded = complete[0].take_next(total)
            slots.note(total)
        slots.close()
        for pair in [pair for pair in reduces if pair[0].done == n_ring - 1]:
            gathers.append(Gather(pair[0].total, pair[1]))
            reduces.remove(pair)
        if opened:
            reduces.append(opened)
        number += 1
    factor = rms_target * math.sqrt(m_total) / (jnp.sqrt(sumsq) + 1e-07)
    factor_sq = factor * factor
    scale = factor_sq.reshape(1)
    for gather in gathers:
        gather.share()
    slots.close()
    for gather in gathers:
        gather.share(False)
    for gather in gathers:
        while not gather.taken:
            total, rounded = gather.take_next(total, scale if gather is gathers[-1] else None)

    def product(d, value):
        return jnp.dot(blocks[d], value, preferred_element_type=F32)

    left, right = slice(0, wide), slice(wide, 2 * wide)
    last = 0.0
    for d in [0, *distances]:
        value = after(flat(mixed[d] if d else own2), rounded[0])
        last = last + product(d, value[:, right])
    first = [total, last * factor_sq]
    rounds = [rounded[0].reshape(2, tall, wide), first[1].astype(BF16).reshape(2, tall, wide)]
    scale_out = 0.2 * math.sqrt(max(m_total, n_in))
    def send(value, *ties):
        value = after(value, *ties) if ties else value
        return {d: across(value, d) for d in near}

    def forward(found, tie):
        if n_row != 4:
            return ()
        one, two = after(found[1][0], tie), after(found[2][1], tie)
        return across(one, 2), across(two, 1)

    def nearby(value, found, tie):
        second = product(0, flat(after(value, tie)))
        for d in near:
            second = second + product(d, flat(swapped(*[after(v, tie) for v in found[d]], d)))
        return second

    def finish(side, second, corner, *ties):
        if corner:
            second = second + product(3, flat(swapped(*[after(v, *ties) for v in corner], 3)))
        mine = flat(own2)[:, (left, right)[side]].astype(F32)
        result = coef_a * mine + coef_b * first[side] + coef_c * (second * factor_sq)
        return (result * (factor * scale_out)).astype(BF16).reshape(2, n_col, half, wide)

    def send_back(block):
        return lax.all_to_all(block, "col", split_axis=1, concat_axis=1, tiled=True)

    found = [send(rounds[0])]
    ended = lax.optimization_barrier((rounds[1], *found[0].values()))[0]
    corner = forward(found[0], ended)
    second = nearby(rounds[0], found[0], ended)
    ended = lax.optimization_barrier((second, *corner))[0]
    found.append(send(rounds[1], ended))
    block = finish(0, second, corner, ended)
    ended = lax.optimization_barrier((block, *found[1].values()))[0]
    backs = [send_back(block)]
    corner = forward(found[1], ended)
    second = nearby(rounds[1], found[1], ended)
    ended = lax.optimization_barrier((second, backs[0], *corner))[0]
    backs.append(send_back(finish(1, second, corner, ended)))
    update = jnp.zeros((rows, n_in), BF16)
    for side, back in enumerate(backs):
        for source in range(n_col):
            piece = back[:, source].reshape(rows, wide)
            update = lax.dynamic_update_slice(update, piece, (0, source * width + side * wide))
    return (update, new_momentum)


def solution(mesh):
    return jax.shard_map(
        shards,
        mesh=mesh,
        in_specs=(P(("row", "col"), None), P(("row", "col"), None)),
        out_specs=(P(("row", "col"), None), P(("row", "col"), None)),
        check_vma=False,
    )
```

time: 1110 us -> 728 us (0.66)
  waiting for transfers between devices: 740 us -> 353 us
  blocking collectives: 210 us -> 0 us
  starting transfers between devices: 0.39 us -> 124 us
  Pallas kernels: 0 us -> 58.1 us
  local copies, waits for them, and re-layouts: 6.49 us -> 39.8 us
  matrix products: 115 us -> 97.3 us
  other arithmetic: 19.1 us -> 36.6 us
    all_gather x3 -> x0, waiting for transfers between devices: 500 us -> none  [the longest x1 222 us: shards(): gram_panel = lax.all_gather(joined, 'col', axis=0, tiled=True)]
    ppermute x0 -> x89, waiting for transfers between devices: none -> 252 us  [the longest x32 126 us: across(): return lax.ppermute(value, 'row', xor_pairs(n_row, distance))]
    reduce_scatter x2 -> x0, waiting for transfers between devices: 240 us -> none  [shards(): lax.psum_scatter(gram_term_rows(jnp.int32(0), share_rows * lax.axis_size(...]
    all_to_all x2 -> x0, blocking collectives: 170 us -> none  [the longest x1 84.9 us: shards(): lax.all_to_all(update_block, 'col', split_axis=0, concat_axis=1, tiled=True)]
    all_to_all x0 -> x4, waiting for transfers between devices: none -> 101 us  [the longest x2 68.2 us: shards(): block = lax.all_to_all(raw_halves[h], 'col', split_axis=0, concat_axis=0)]
    ppermute x0 -> x89, starting transfers between devices: none -> 89.9 us  [the longest x37 34.8 us: other_core(): return lax.ppermute(value, 'col', xor_pairs(n_col, 1))]
    pallas_call x0 -> x5, Pallas kernels: none -> 58.1 us  [the longest x4 48.1 us: absorb(): pl.pallas_call(functools.partial(absorb_kernel, len(near) // 2, half, fir...]
    psum x1 -> x0, blocking collectives: 40.1 us -> none  [shards(): sumsq = lax.psum(jnp.sum(direction * direction), ('row', 'col'))]
  transfers between devices with their start and end apart: 5 -> 93, of which waited for: 5 -> 41; matrix products, arithmetic and copies ran while one was open for 2% -> 18% of each run, Pallas kernels for 0% -> 5%
where the time goes in v2:
time: 728 us; the launch traced here: 714 us
  waiting for transfers between devices  353 us (48%)
  starting transfers between devices  124 us (17%)
  matrix products  97.3 us (13%)
  Pallas kernels  58.1 us (8%)
  local copies, waits for them, and re-layouts  39.8 us (5%)
  other arithmetic  36.6 us (5%)
    ppermute x32, waiting for transfers between devices, across(): return lax.ppermute(value, 'row', xor_pairs(n_row, distance))  126 us
    ppermute x18, waiting for transfers between devices, next_in_ring(): return lax.ppermute(value, 'col', shift_pairs(n_col, 2))  117 us
    dot_general x12, matrix products, product(): return jnp.dot(blocks[d], value, preferred_element_type=F32)  73.7 us
    all_to_all x2, waiting for transfers between devices, shards(): block = lax.all_to_all(raw_halves[h], 'col', split_axis=0, concat_axis=0)  68.2 us
    pallas_call x4, Pallas kernels, absorb(): pl.pallas_call(functools.partial(absorb_kernel, len(near) // 2, half, fir...  48.1 us
    ppermute x37, starting transfers between devices, other_core(): return lax.ppermute(value, 'col', xor_pairs(n_col, 1))  34.8 us
    all_to_all x2, waiting for transfers between devices, send_back(): return lax.all_to_all(block, 'col', split_axis=1, concat_axis=1, tiled=True)  32.6 us
    ppermute x32, starting transfers between devices, across(): return lax.ppermute(value, 'row', xor_pairs(n_row, distance))  31.7 us
  transfers between devices with their start and end apart: 93, of which 41 were waited for; matrix products, arithmetic and copies ran while one was open for 18% of the time, Pallas kernels for 5%

profile of v2, /device:TPU:9, one launch (start us, length us, event | category | flops | bytes accessed | tf_op | source)
XLA Modules:
  0.0 714.5 jit_solution(568418995621733151)
XLA Ops:
  0.6 10.0 %shard_map.41 = (f32[224,8192]{1,0:T(8,128)}, bf16[8,112,1024]{2,1,0:T(8,128)(2,1)}, bf16[8,112,1024]{2,1,0:T(8,128)(2,1)}, f32[1,1]{1,0:T(1,128)}) custom-call(f32[224,8192]{1,0:T(8,128)} %grad.1, f32[224,8192]{1,0:T(8,128)} %momentum.1), custom_call_target="tpu_custom_call" | custom-call | tf_op jit(solution)/shard_map/pallas_call | solution.py:92
  25.4 30.7 %all-to-all-done = bf16[8,112,1024]{2,1,0:T(8,128)(2,1)S(1)} async-done(((bf16[8,112,1024]{2,1,0:T(8,128)(2,1)}), bf16[8,112,1024]{2,1,0:T(8,128)(2,1)S(1)}, u32[]{:S(2)}, u32[]{:S(2)}) %all-to-all-start) | async-done | bytes 1835040 | tf_op jit(solution)/shard_map/all_to_all | solution.py:252
  67.0 37.4 %all-to-all-done.1 = bf16[8,112,1024]{2,1,0:T(8,128)(2,1)S(1)} async-done(((bf16[8,112,1024]{2,1,0:T(8,128)(2,1)}), bf16[8,112,1024]{2,1,0:T(8,128)(2,1)S(1)}, u32[]{:S(2)}, u32[]{:S(2)}) %all-to-all-start.1) | async-done | bytes 1835040 | tf_op jit(solution)/shard_map/all_to_all | solution.py:252
  123.3 8.6 %collective-permute-done.5 = bf16[448,1024]{1,0:T(8,128)(2,1)S(1)} collective-permute-done((bf16[448,1024]{1,0:T(8,128)(2,1)S(1)}, bf16[448,1024]{1,0:T(8,128)(2,1)S(1)}, u32[]{:S(2)}, u32[]{:S(2)}) %collective-permute-start.5) | collective-permute-done | bytes 917536 | tf_op jit(solution)/shard_map/ppermute | solution.py:232
  225.1 29.0 %collective-permute-done.31.refs_3_ = bf16[3,112,896]{2,1,0:T(8,128)(2,1)S(1)} collective-permute-done((bf16[3,112,896]{2,1,0:T(8,128)(2,1)S(1)}, bf16[3,112,896]{2,1,0:T(8,128)(2,1)S(1)}, u32[]{:S(2)}, u32[]{:S(2)}) %collective-permute-start.31) | collective-permute-done | bytes 602144 | tf_op jit(solution)/shard_map/ppermute | solution.py:238
  261.9 21.7 %collective-permute-done.35 = bf16[2,112,896]{2,1,0:T(8,128)(2,1)S(1)} collective-permute-done((bf16[2,112,896]{2,1,0:T(8,128)(2,1)S(1)}, bf16[2,112,896]{2,1,0:T(8,128)(2,1)S(1)}, u32[]{:S(2)}, u32[]{:S(2)}) %collective-permute-start.35) | collective-permute-done | bytes 401440 | tf_op jit(solution)/shard_map/ppermute | solution.py:238
  284.5 12.1 %collective-permute-done.38.refs_4_ = bf16[3,112,896]{2,1,0:T(8,128)(2,1)} collective-permute-done((bf16[3,112,896]{2,1,0:T(8,128)(2,1)S(1)}, bf16[3,112,896]{2,1,0:T(8,128)(2,1)}, u32[]{:S(2)}, u32[]{:S(2)}) %collective-permute-start.38) | collective-permute-done | bytes 602144 | tf_op jit(solution)/shard_map/ppermute | solution.py:238
  312.4 10.7 %shard_map.42 = (bf16[1792,1792]{1,0:T(8,128)(2,1)}, f32[1792,512]{1,0:T(8,128)}) custom-call(s32[8]{0:T(128)} %stack.124.refs_0_, bf16[3,112,896]{2,1,0:T(8,128)(2,1)} %copy-done.41, bf16[3,112,896]{2,1,0:T(8,128)(2,1)} %copy-done.70, bf16[3,112,896]{2,1,0:T(8,128)(2,1)} %copy-done.72, bf16[3,112,896]{2,1,0:T(8,128)(2,1)} %collective-permute-done.38.refs_4_, ...), custom_call_target="tpu_custom_call" | custom-call | flops 3288334336 | bytes 24084480 | tf_op jit(solution)/shard_map/pallas_call | solution.py:191
  334.7 24.6 %collective-permute-done.42 = bf16[2,112,896]{2,1,0:T(8,128)(2,1)S(1)} collective-permute-done((bf16[2,112,896]{2,1,0:T(8,128)(2,1)S(1)}, bf16[2,112,896]{2,1,0:T(8,128)(2,1)S(1)}, u32[]{:S(2)}, u32[]{:S(2)}) %collective-permute-start.42) | collective-permute-done | bytes 401440 | tf_op jit(solution)/shard_map/ppermute | solution.py:238
  363.0 9.1 %collective-permute-done.47.refs_10_ = bf16[2,112,896]{2,1,0:T(8,128)(2,1)S(1)} collective-permute-done((bf16[2,112,896]{2,1,0:T(8,128)(2,1)S(1)}, bf16[2,112,896]{2,1,0:T(8,128)(2,1)S(1)}, u32[]{:S(2)}, u32[]{:S(2)}) %collective-permute-start.47) | collective-permute-done | bytes 401440 | tf_op jit(solution)/shard_map/ppermute | solution.py:232
  375.2 17.2 %collective-permute-done.51.refs_10_ = bf16[2,112,896]{2,1,0:T(8,128)(2,1)S(1)} collective-permute-done((bf16[2,112,896]{2,1,0:T(8,128)(2,1)S(1)}, bf16[2,112,896]{2,1,0:T(8,128)(2,1)S(1)}, u32[]{:S(2)}, u32[]{:S(2)}) %collective-permute-start.51) | collective-permute-done | bytes 401440 | tf_op jit(solution)/shard_map/ppermute | solution.py:232
  444.9 12.5 %shard_map.43 = (bf16[1792,1792]{1,0:T(8,128)(2,1)}, f32[1792,512]{1,0:T(8,128)}) custom-call(s32[8]{0:T(128)} %stack.124.refs_0_, bf16[4,112,896]{2,1,0:T(8,128)(2,1)} %copy-done.3, bf16[4,112,896]{2,1,0:T(8,128)(2,1)} %copy-done.19, bf16[4,112,896]{2,1,0:T(8,128)(2,1)} %copy-done.20, bf16[4,112,896]{2,1,0:T(8,128)(2,1)} %copy-done.21, ...), custom_call_target="tpu_custom_call" | custom-call | flops 3288334336 | bytes 24084480 | tf_op jit(solution)/shard_map/pallas_call | solution.py:191
  463.2 12.6 %shard_map.44 = (bf16[1792,1792]{1,0:T(8,128)(2,1)}, f32[1792,512]{1,0:T(8,128)}) custom-call(s32[8]{0:T(128)} %stack.124.refs_0_, bf16[4,112,896]{2,1,0:T(8,128)(2,1)} %copy-done.3, bf16[4,112,896]{2,1,0:T(8,128)(2,1)} %copy-done.19, bf16[4,112,896]{2,1,0:T(8,128)(2,1)} %copy-done.20, bf16[4,112,896]{2,1,0:T(8,128)(2,1)} %copy-done.21, ...), custom_call_target="tpu_custom_call" | custom-call | flops 3288334336 | bytes 24084480 | tf_op jit(solution)/shard_map/pallas_call | solution.py:191
  478.2 8.8 %collective-permute-done.78.refs_13_ = bf16[2,112,896]{2,1,0:T(8,128)(2,1)S(1)} collective-permute-done((bf16[2,112,896]{2,1,0:T(8,128)(2,1)S(1)}, bf16[2,112,896]{2,1,0:T(8,128)(2,1)S(1)}, u32[]{:S(2)}, u32[]{:S(2)}) %collective-permute-start.78) | collective-permute-done | bytes 401440 | tf_op jit(solution)/shard_map/ppermute | solution.py:232
  492.0 12.4 %shard_map.45 = (bf16[1792,1792]{1,0:T(8,128)(2,1)}, f32[1792,512]{1,0:T(8,128)}, bf16[1792,512]{1,0:T(8,128)(2,1)}) custom-call(s32[8]{0:T(128)} %stack.124.refs_0_, f32[1]{0:T(128)} %bitcast.31.refs_1_, bf16[2,112,896]{2,1,0:T(8,128)(2,1)} %copy-done.24, bf16[2,112,896]{2,1,0:T(8,128)(2,1)} %copy-done.30, bf16[2,112,896]{2,1,0:T(8,128)(2,1)} %copy-done.31, ...), custom_call_target="tpu_custom_call" | custom-call | flops 3288334336 | bytes 24084480 | tf_op jit(solution)/shard_map/pallas_call | solution.py:191
  506.0 8.3 %fusion.1 = f32[1792,512]{1,0:T(8,128)} fusion(bf16[1792,1792]{1,0:T(8,128)(2,1)} %get-tuple-element.194, bf16[1792,1024]{1,0:T(8,128)(2,1)S(1)} %bitcast.236), kind=kOutput, calls=%fused_computation.24 | convolution fusion | flops 3288334336 | bytes 11927552 | tf_op jit(solution)/shard_map/dot_general | solution.py:462
  514.3 8.3 %fusion.5 = f32[1792,512]{1,0:T(8,128)} fusion(bf16[1792,1792]{1,0:T(8,128)(2,1)} %get-tuple-element.189, bf16[1792,1024]{1,0:T(8,128)(2,1)S(1)} %bitcast.248), kind=kOutput, calls=%fused_computation.28 | convolution fusion | flops 3288334336 | bytes 11927552 | tf_op jit(solution)/shard_map/dot_general | solution.py:462
  528.1 8.4 %fusion.17 = (bf16[1792,512]{1,0:T(8,128)(2,1)}, f32[1792,512]{1,0:T(8,128)}) fusion(f32[]{:T(128)} %bitcast.69, bf16[1792,1792]{1,0:T(8,128)(2,1)S(1)} %bitcast.291, bf16[1792,1024]{1,0:T(8,128)(2,1)S(1)} %bitcast.238, f32[1792,512]{1,0:T(8,128)} %fusion.1, f32[1792,512]{1,0:T(8,128)} %fusion.5, f32[1792,512]{1,0:T(8,128)} %fusion.3), kind=kOutput, calls=%fused_computation.159 | convolution fusion | flops 3292921856 | bytes 24772612 | tf_op jit(solution)/shard_map/dot_general | solution.py:462
  536.5 9.8 %collective-permute-done.81 = bf16[2,896,512]{2,1,0:T(8,128)(2,1)S(1)} collective-permute-done((bf16[2,896,512]{2,1,0:T(8,128)(2,1)}, bf16[2,896,512]{2,1,0:T(8,128)(2,1)S(1)}, u32[]{:S(2)}, u32[]{:S(2)}) %collective-permute-start.81) | collective-permute-done | bytes 1835040 | tf_op jit(solution)/shard_map/ppermute | solution.py:232
  567.0 12.8 %collective-permute-done.83 = bf16[896,512]{1,0:T(8,128)(2,1)S(1)} collective-permute-done((bf16[896,512]{1,0:T(8,128)(2,1)S(1)}, bf16[896,512]{1,0:T(8,128)(2,1)S(1)}, u32[]{:S(2)}, u32[]{:S(2)}) %collective-permute-start.83) | collective-permute-done | bytes 917536 | tf_op jit(solution)/shard_map/ppermute | solution.py:232
  590.4 9.7 %all-to-all-start.2 = ((bf16[2,8,112,512]{3,2,0,1:T(8,128)(2,1)}), bf16[2,8,112,512]{3,2,0,1:T(8,128)(2,1)S(1)}, u32[]{:S(2)}, u32[]{:S(2)}) async-start(bf16[2,8,112,512]{3,2,0,1:T(8,128)(2,1)} %copy.84), calls=%async_computation.2 | async-start | bytes 3670016 | tf_op jit(solution)/shard_map/all_to_all | solution.py:496
  600.1 19.3 %collective-permute-done.85 = bf16[2,896,512]{2,1,0:T(8,128)(2,1)} collective-permute-done((bf16[2,896,512]{2,1,0:T(8,128)(2,1)}, bf16[2,896,512]{2,1,0:T(8,128)(2,1)}, u32[]{:S(2)}, u32[]{:S(2)}) %collective-permute-start.85) | collective-permute-done | bytes 1835040 | tf_op jit(solution)/shard_map/ppermute | solution.py:232
  655.6 11.3 %all-to-all-start.3 = ((bf16[2,8,112,512]{3,2,0,1:T(8,128)(2,1)}), bf16[2,8,112,512]{3,2,0,1:T(8,128)(2,1)}, u32[]{:S(2)}, u32[]{:S(2)}) async-start(bf16[2,8,112,512]{3,2,0,1:T(8,128)(2,1)} %copy.85), calls=%async_computation.3 | async-start | bytes 3670016 | tf_op jit(solution)/shard_map/all_to_all | solution.py:496
  674.1 32.6 %all-to-all-done.3 = bf16[2,8,112,512]{3,2,0,1:T(8,128)(2,1)} async-done(((bf16[2,8,112,512]{3,2,0,1:T(8,128)(2,1)}), bf16[2,8,112,512]{3,2,0,1:T(8,128)(2,1)}, u32[]{:S(2)}, u32[]{:S(2)}) %all-to-all-start.3) | async-done | bytes 1835040 | tf_op jit(solution)/shard_map/all_to_all | solution.py:496
  (466 shorter events, 330.2 us)
Async XLA Ops:
  10.6 45.5 %all-to-all-start = ((bf16[8,112,1024]{2,1,0:T(8,128)(2,1)}), bf16[8,112,1024]{2,1,0:T(8,128)(2,1)S(1)}, u32[]{:S(2)}, u32[]{:S(2)}) async-start(bf16[8,112,1024]{2,1,0:T(8,128)(2,1)} %get-tuple-element.110), calls=%async_computation | async-start | bytes 3670016 | tf_op jit(solution)/shard_map/all_to_all | solution.py:252
  57.5 46.9 %all-to-all-start.1 = ((bf16[8,112,1024]{2,1,0:T(8,128)(2,1)}), bf16[8,112,1024]{2,1,0:T(8,128)(2,1)S(1)}, u32[]{:S(2)}, u32[]{:S(2)}) async-start(bf16[8,112,1024]{2,1,0:T(8,128)(2,1)} %get-tuple-element.113), calls=%async_computation.1 | async-start | bytes 3670016 | tf_op jit(solution)/shard_map/all_to_all | solution.py:252
  64.5 41.6 %collective-permute-start.3 = (bf16[896,1024]{1,0:T(8,128)(2,1)}, bf16[896,1024]{1,0:T(8,128)(2,1)}, u32[]{:S(2)}, u32[]{:S(2)}) collective-permute-start(bf16[896,1024]{1,0:T(8,128)(2,1)} %bitcast.239), channel_id=1, source_target_pairs={{0,8},{8,0},{16,24},{24,16},{1,9},{9,1},{17,25},{25,17},{2,10},{10... | collective-permute-start | bytes 5505032 | tf_op jit(solution)/shard_map/ppermute | solution.py:232
  65.7 41.2 %collective-permute-start.4 = (bf16[896,1024]{1,0:T(8,128)(2,1)}, bf16[896,1024]{1,0:T(8,128)(2,1)}, u32[]{:S(2)}, u32[]{:S(2)}) collective-permute-start(bf16[896,1024]{1,0:T(8,128)(2,1)} %bitcast.240), channel_id=1, source_target_pairs={{0,16},{8,24},{16,0},{24,8},{1,17},{9,25},{17,1},{25,9},{2,18},{10... | collective-permute-start | bytes 5505032 | tf_op jit(solution)/shard_map/ppermute | solution.py:232
  123.3 34.1 %collective-permute-start.8 = (bf16[3,112,896]{2,1,0:T(8,128)(2,1)}, bf16[3,112,896]{2,1,0:T(8,128)(2,1)}, u32[]{:S(2)}, u32[]{:S(2)}) collective-permute-start(bf16[3,112,896]{2,1,0:T(8,128)(2,1)} %pad_maximum_fusion.19), channel_id=1, source_target_pairs={{0,1},{1,0},{2,3},{3,2},{4,5},{5,4},{6,7},{7,6},{8,9},{9,8},{10,11... | collective-permute-start | bytes 1806344 | tf_op jit(solution)/shard_map/ppermute | solution.py:235
  157.5 33.9 %collective-permute-start.10 = (bf16[3,112,896]{2,1,0:T(8,128)(2,1)S(1)}, bf16[3,112,896]{2,1,0:T(8,128)(2,1)S(1)}, u32[]{:S(2)}, u32[]{:S(2)}) collective-permute-start(bf16[3,112,896]{2,1,0:T(8,128)(2,1)S(1)} %pad_maximum_fusion.21), channel_id=1, source_target_pairs={{0,1},{1,0},{2,3},{3,2},{4,5},{5,4},{6,7},{7,6},{8,9},{9,8},{10,11... | collective-permute-start | bytes 1806344 | tf_op jit(solution)/shard_map/ppermute | solution.py:235
  220.4 33.7 %collective-permute-start.30 = (bf16[4,112,896]{2,1,0:T(8,128)(2,1)S(1)}, bf16[4,112,896]{2,1,0:T(8,128)(2,1)S(1)}, u32[]{:S(2)}, u32[]{:S(2)}) collective-permute-start(bf16[4,112,896]{2,1,0:T(8,128)(2,1)S(1)} %fusion.8), channel_id=1, source_target_pairs={{0,2},{1,3},{2,4},{3,5},{4,6},{5,7},{6,0},{7,1},{8,10},{9,11},{10,... | collective-permute-start | bytes 2408456 | tf_op jit(solution)/shard_map/ppermute | solution.py:238
  220.8 33.4 %collective-permute-start.25 = (bf16[4,112,896]{2,1,0:T(8,128)(2,1)S(1)}, bf16[4,112,896]{2,1,0:T(8,128)(2,1)S(1)}, u32[]{:S(2)}, u32[]{:S(2)}) collective-permute-start(bf16[4,112,896]{2,1,0:T(8,128)(2,1)S(1)} %pad_maximum_fusion.15), channel_id=1, source_target_pairs={{0,1},{1,0},{2,3},{3,2},{4,5},{5,4},{6,7},{7,6},{8,9},{9,8},{10,11... | collective-permute-start | bytes 2408456 | tf_op jit(solution)/shard_map/ppermute | solution.py:235
  221.6 32.5 %collective-permute-start.31 = (bf16[3,112,896]{2,1,0:T(8,128)(2,1)S(1)}, bf16[3,112,896]{2,1,0:T(8,128)(2,1)S(1)}, u32[]{:S(2)}, u32[]{:S(2)}) collective-permute-start(bf16[3,112,896]{2,1,0:T(8,128)(2,1)S(1)} %collective-permute-done.23.refs_2_), channel_id=1, source_target_pairs={{0,2},{1,3},{2,4},{3,5},{4,6},{5,7},{6,0},{7,1},{8,10},{9,11},{10,... | collective-permute-start | bytes 1806344 | tf_op jit(solution)/shard_map/ppermute | solution.py:238
  222.6 31.5 %collective-permute-start.29 = (bf16[3,112,896]{2,1,0:T(8,128)(2,1)S(1)}, bf16[3,112,896]{2,1,0:T(8,128)(2,1)S(1)}, u32[]{:S(2)}, u32[]{:S(2)}) collective-permute-start(bf16[3,112,896]{2,1,0:T(8,128)(2,1)S(1)} %collective-permute-done.23.refs_2_), channel_id=1, source_target_pairs={{0,1},{1,0},{2,3},{3,2},{4,5},{5,4},{6,7},{7,6},{8,9},{9,8},{10,11... | collective-permute-start | bytes 1806344 | tf_op jit(solution)/shard_map/ppermute | solution.py:235
  254.4 42.2 %collective-permute-start.37 = (bf16[4,112,896]{2,1,0:T(8,128)(2,1)S(1)}, bf16[4,112,896]{2,1,0:T(8,128)(2,1)S(1)}, u32[]{:S(2)}, u32[]{:S(2)}) collective-permute-start(bf16[4,112,896]{2,1,0:T(8,128)(2,1)S(1)} %add_convert_fusion.2), channel_id=1, source_target_pairs={{0,2},{1,3},{2,4},{3,5},{4,6},{5,7},{6,0},{7,1},{8,10},{9,11},{10,... | collective-permute-start | bytes 2408456 | tf_op jit(solution)/shard_map/ppermute | solution.py:238
  254.6 43.5 %collective-permute-start.26 = (bf16[4,112,896]{2,1,0:T(8,128)(2,1)S(1)}, bf16[4,112,896]{2,1,0:T(8,128)(2,1)S(1)}, u32[]{:S(2)}, u32[]{:S(2)}) collective-permute-start(bf16[4,112,896]{2,1,0:T(8,128)(2,1)S(1)} %pad_maximum_fusion.16), channel_id=1, source_target_pairs={{0,1},{1,0},{2,3},{3,2},{4,5},{5,4},{6,7},{7,6},{8,9},{9,8},{10,11... | collective-permute-start | bytes 2408456 | tf_op jit(solution)/shard_map/ppermute | solution.py:235
  257.2 39.4 %collective-permute-start.38 = (bf16[3,112,896]{2,1,0:T(8,128)(2,1)S(1)}, bf16[3,112,896]{2,1,0:T(8,128)(2,1)}, u32[]{:S(2)}, u32[]{:S(2)}) collective-permute-start(bf16[3,112,896]{2,1,0:T(8,128)(2,1)S(1)} %collective-permute-done.31.refs_3_), channel_id=1, source_target_pairs={{0,2},{1,3},{2,4},{3,5},{4,6},{5,7},{6,0},{7,1},{8,10},{9,11},{10,... | collective-permute-start | bytes 1806344 | tf_op jit(solution)/shard_map/ppermute | solution.py:238
  261.2 35.4 %collective-permute-start.36 = (bf16[3,112,896]{2,1,0:T(8,128)(2,1)S(1)}, bf16[3,112,896]{2,1,0:T(8,128)(2,1)S(1)}, u32[]{:S(2)}, u32[]{:S(2)}) collective-permute-start(bf16[3,112,896]{2,1,0:T(8,128)(2,1)S(1)} %collective-permute-done.31.refs_3_), channel_id=1, source_target_pairs={{0,1},{1,0},{2,3},{3,2},{4,5},{5,4},{6,7},{7,6},{8,9},{9,8},{10,11... | collective-permute-start | bytes 1806344 | tf_op jit(solution)/shard_map/ppermute | solution.py:235
  330.2 29.3 %collective-permute-start.43 = (bf16[4,112,896]{2,1,0:T(8,128)(2,1)S(1)}, bf16[4,112,896]{2,1,0:T(8,128)(2,1)S(1)}, u32[]{:S(2)}, u32[]{:S(2)}) collective-permute-start(bf16[4,112,896]{2,1,0:T(8,128)(2,1)S(1)} %add_convert_fusion.refs_1_), channel_id=1, source_target_pairs={{0,2},{1,3},{2,4},{3,5},{4,6},{5,7},{6,0},{7,1},{8,10},{9,11},{10,... | collective-permute-start | bytes 2408456 | tf_op jit(solution)/shard_map/ppermute | solution.py:238
  330.3 29.2 %collective-permute-start.44 = (bf16[4,112,896]{2,1,0:T(8,128)(2,1)S(1)}, bf16[4,112,896]{2,1,0:T(8,128)(2,1)S(1)}, u32[]{:S(2)}, u32[]{:S(2)}) collective-permute-start(bf16[4,112,896]{2,1,0:T(8,128)(2,1)S(1)} %add_convert_fusion.refs_1_), channel_id=1, source_target_pairs={{0,1},{1,0},{2,3},{3,2},{4,5},{5,4},{6,7},{7,6},{8,9},{9,8},{10,11... | collective-permute-start | bytes 2408456 | tf_op jit(solution)/shard_map/ppermute | solution.py:235
  359.5 33.0 %collective-permute-start.50 = (bf16[4,112,896]{2,1,0:T(8,128)(2,1)S(1)}, bf16[4,112,896]{2,1,0:T(8,128)(2,1)S(1)}, u32[]{:S(2)}, u32[]{:S(2)}) collective-permute-start(bf16[4,112,896]{2,1,0:T(8,128)(2,1)S(1)} %collective-permute-done.43.refs_2_), channel_id=1, source_target_pairs={{0,1},{1,0},{2,3},{3,2},{4,5},{5,4},{6,7},{7,6},{8,9},{9,8},{10,11... | collective-permute-start | bytes 2408456 | tf_op jit(solution)/shard_map/ppermute | solution.py:235
  361.0 31.5 %collective-permute-start.54 = (bf16[4,112,896]{2,1,0:T(8,128)(2,1)S(1)}, bf16[4,112,896]{2,1,0:T(8,128)(2,1)S(1)}, u32[]{:S(2)}, u32[]{:S(2)}) collective-permute-start(bf16[4,112,896]{2,1,0:T(8,128)(2,1)S(1)} %collective-permute-done.43.refs_2_), channel_id=1, source_target_pairs={{0,2},{1,3},{2,4},{3,5},{4,6},{5,7},{6,0},{7,1},{8,10},{9,11},{10,... | collective-permute-start | bytes 2408456 | tf_op jit(solution)/shard_map/ppermute | solution.py:238
  504.4 41.9 %collective-permute-start.81 = (bf16[2,896,512]{2,1,0:T(8,128)(2,1)}, bf16[2,896,512]{2,1,0:T(8,128)(2,1)S(1)}, u32[]{:S(2)}, u32[]{:S(2)}) collective-permute-start(bf16[2,896,512]{2,1,0:T(8,128)(2,1)} %bitcast.294), channel_id=1, source_target_pairs={{0,8},{8,0},{16,24},{24,16},{1,9},{9,1},{17,25},{25,17},{2,10},{10... | collective-permute-start | bytes 5505032 | tf_op jit(solution)/shard_map/ppermute | solution.py:232
  505.6 41.5 %collective-permute-start.82 = (bf16[2,896,512]{2,1,0:T(8,128)(2,1)}, bf16[2,896,512]{2,1,0:T(8,128)(2,1)S(1)}, u32[]{:S(2)}, u32[]{:S(2)}) collective-permute-start(bf16[2,896,512]{2,1,0:T(8,128)(2,1)} %bitcast.295), channel_id=1, source_target_pairs={{0,16},{8,24},{16,0},{24,8},{1,17},{9,25},{17,1},{25,9},{2,18},{10... | collective-permute-start | bytes 5505032 | tf_op jit(solution)/shard_map/ppermute | solution.py:232
  579.8 39.5 %collective-permute-start.85 = (bf16[2,896,512]{2,1,0:T(8,128)(2,1)}, bf16[2,896,512]{2,1,0:T(8,128)(2,1)}, u32[]{:S(2)}, u32[]{:S(2)}) collective-permute-start(bf16[2,896,512]{2,1,0:T(8,128)(2,1)} %bitcast.70), channel_id=1, source_target_pairs={{0,8},{8,0},{16,24},{24,16},{1,9},{9,1},{17,25},{25,17},{2,10},{10... | collective-permute-start | bytes 5505032 | tf_op jit(solution)/shard_map/ppermute | solution.py:232
  580.2 39.2 %collective-permute-start.86 = (bf16[2,896,512]{2,1,0:T(8,128)(2,1)}, bf16[2,896,512]{2,1,0:T(8,128)(2,1)}, u32[]{:S(2)}, u32[]{:S(2)}) collective-permute-start(bf16[2,896,512]{2,1,0:T(8,128)(2,1)} %bitcast.70), channel_id=1, source_target_pairs={{0,16},{8,24},{16,0},{24,8},{1,17},{9,25},{17,1},{25,9},{2,18},{10... | collective-permute-start | bytes 5505032 | tf_op jit(solution)/shard_map/ppermute | solution.py:232
  590.4 52.7 %all-to-all-start.2 = ((bf16[2,8,112,512]{3,2,0,1:T(8,128)(2,1)}), bf16[2,8,112,512]{3,2,0,1:T(8,128)(2,1)S(1)}, u32[]{:S(2)}, u32[]{:S(2)}) async-start(bf16[2,8,112,512]{3,2,0,1:T(8,128)(2,1)} %copy.84), calls=%async_computation.2 | async-start | bytes 3670016 | tf_op jit(solution)/shard_map/all_to_all | solution.py:496
  655.6 51.2 %all-to-all-start.3 = ((bf16[2,8,112,512]{3,2,0,1:T(8,128)(2,1)}), bf16[2,8,112,512]{3,2,0,1:T(8,128)(2,1)}, u32[]{:S(2)}, u32[]{:S(2)}) async-start(bf16[2,8,112,512]{3,2,0,1:T(8,128)(2,1)} %copy.85), calls=%async_computation.3 | async-start | bytes 3670016 | tf_op jit(solution)/shard_map/all_to_all | solution.py:496
  (161 other events, 2856.1 us)

commit v3 on v2

--- a/solution.py
+++ b/solution.py
@@ -49,23 +49,19 @@
             self.noted = []
 
 
-def direction_kernel(grad, momentum, new_momentum, upper, lower, sumsq, squares):
-    lower_half, part = pl.program_id(0), pl.program_id(1)
+def direction_kernel(grad, momentum, *refs):
+    new_momentum, raw, sumsq, squares = refs[-4:]
+    part = pl.program_id(0)
     state = momentum_coef * momentum[...] + grad[...]
     new_momentum[...] = state
     direction = grad[...] + momentum_coef * state
-    width = upper.shape[2]
-
-    @pl.when((lower_half == 0) & (part == 0))
+    width = raw.shape[2]
+    for group in range(raw.shape[0]):
+        raw[group] = direction[:, group * width : (group + 1) * width].astype(BF16)
+
+    @pl.when(part == 0)
     def _():
         squares[...] = jnp.zeros_like(squares)
-
-    for out, mine in ((upper, lower_half == 0), (lower, lower_half == 1)):
-
-        @pl.when(mine)
-        def _(out=out):
-            for group in range(out.shape[0]):
-                out[group] = direction[:, group * width : (group + 1) * width].astype(BF16)
 
     total = squares[...]
     for row in range(0, direction.shape[0], 8):
@@ -73,9 +69,35 @@
         total = total + rows * rows
     squares[...] = total
 
-    @pl.when((lower_half == 1) & (part == pl.num_programs(1) - 1))
+    @pl.when(part == pl.num_programs(0) - 1)
     def _():
         sumsq[0, 0] = jnp.sum(squares[...])
+
+
+def direction_half(grad, momentum, n_col, lower, state):
+    rows, n_in = grad.shape
+    half, width = rows // 2, n_in // n_col
+    parts = 2
+    tile = pl.BlockSpec((half, n_in // parts), lambda j: (lower, j))
+    filled = [] if state is None else [state]
+    return pl.pallas_call(
+        direction_kernel,
+        grid=(parts,),
+        in_specs=[tile, tile] + [pl.BlockSpec(memory_space=pl.ANY)] * len(filled),
+        out_specs=[
+            tile,
+            pl.BlockSpec((n_col // parts, half, width), lambda j: (j, 0, 0)),
+            pl.BlockSpec(memory_space=pltpu.SMEM),
+        ],
+        out_shape=[
+            jax.ShapeDtypeStruct((rows, n_in), F32),
+            jax.ShapeDtypeStruct((n_col, half, width), BF16),
+            jax.ShapeDtypeStruct((1, 1), F32),
+        ],
+        input_output_aliases={2: 0} if filled else {},
+        scratch_shapes=[pltpu.VMEM((8, n_in // parts), F32)],
+        compiler_params=pltpu.CompilerParams(vmem_limit_bytes=VMEM),
+    )(grad, momentum, *filled)
 
 
 def direction_step(grad, momentum, n_col):
@@ -86,37 +108,17 @@
         direction = grad + momentum_coef * state
         raw = direction.astype(BF16).reshape(2, half, n_col, width).transpose(0, 2, 1, 3)
         return state, raw[0], raw[1], jnp.sum(direction * direction).reshape(1, 1)
-    parts = 2
-    tile = pl.BlockSpec((half, n_in // parts), lambda i, j: (i, j))
-    groups = (n_col // parts, half, width)
-    return pl.pallas_call(
-        direction_kernel,
-        grid=(2, parts),
-        in_specs=[tile, tile],
-        out_specs=[
-            tile,
-            pl.BlockSpec(groups, lambda i, j: (jnp.where(i == 0, j, parts - 1), 0, 0)),
-            pl.BlockSpec(groups, lambda i, j: (jnp.where(i == 0, 0, j), 0, 0)),
-            pl.BlockSpec(memory_space=pltpu.SMEM),
-        ],
-        out_shape=[
-            jax.ShapeDtypeStruct((rows, n_in), F32),
-            jax.ShapeDtypeStruct((n_col, half, width), BF16),
-            jax.ShapeDtypeStruct((n_col, half, width), BF16),
-            jax.ShapeDtypeStruct((1, 1), F32),
-        ],
-        scratch_shapes=[pltpu.VMEM((8, n_in // parts), F32)],
-        compiler_params=pltpu.CompilerParams(vmem_limit_bytes=VMEM),
-    )(grad, momentum)
-
-
-def absorb_kernel(n_ring, half, first_near, mirrored, seeded, scaled, *refs):
+    state, upper, upper_sum = direction_half(grad, momentum, n_col, 0, None)
+    state, lower, lower_sum = direction_half(grad, momentum, n_col, 1, state)
+    return state, upper, lower, upper_sum + lower_sum
+
+
+def absorb_kernel(half, near_at, far_at, seeded, scaled, *refs):
     places, refs = refs[0], refs[1:]
     if scaled:
         scale, refs = refs[0], refs[1:]
-    near, refs = refs[: 2 * n_ring], refs[2 * n_ring :]
-    if not mirrored:
-        far, refs = refs[: 2 * n_ring], refs[2 * n_ring :]
+    near, refs = refs[: len(near_at)], refs[len(near_at) :]
+    far, refs = refs[: len(far_at)], refs[len(far_at) :]
     value, refs = refs[0], refs[1:]
     if seeded:
         before, refs = refs[0], refs[1:]
@@ -135,20 +137,20 @@
             copy.start()
             copies.append(copy)
 
-        for k in range(2 * n_ring):
+        for k in range(len(near)):
             at = pl.ds(pl.multiple_of(places[k], 16), half)
             below = pl.ds(pl.multiple_of(places[k] + tall, 16), half)
-            place(near[k].at[first_near], block.at[at, pl.ds(0, tall)])
-            place(near[k].at[first_near + 1], block.at[below, pl.ds(tall, tall)])
-            if mirrored:
-                place(near[k].at[first_near + 2], block.at[at, pl.ds(tall, tall)])
+            place(near[k].at[near_at[k]], block.at[at, pl.ds(0, tall)])
+            place(near[k].at[near_at[k] + 1], block.at[below, pl.ds(tall, tall)])
+            if not far:
+                place(near[k].at[near_at[k] + 2], block.at[at, pl.ds(tall, tall)])
             else:
-                place(far[k].at[0], turned.at[0, at])
-                place(far[k].at[1], turned.at[1, at])
+                place(far[k].at[far_at[k]], turned.at[0, at])
+                place(far[k].at[far_at[k] + 1], turned.at[1, at])
         for copy in copies:
             copy.wait()
         for j in range(0, tall, 128):
-            if mirrored:
+            if not far:
                 block[pl.ds(tall + j, 128), pl.ds(0, tall)] = block[
                     pl.ds(0, tall), pl.ds(tall + j, 128)
                 ].T
@@ -165,8 +167,8 @@
     total[...] = result
 
 
-def absorb(places, near, first_near, far, value, wide, before=None, scale=None):
-    _, half, tall = near[0].shape
+def absorb(places, near, far, value, wide, before=None, scale=None):
+    _, half, tall = near[0][0].shape
     tile = min(TILE, wide)
     whole = pl.BlockSpec(memory_space=pl.ANY)
     scalars = pl.BlockSpec(memory_space=pltpu.SMEM)
@@ -175,7 +177,7 @@
     if scale is not None:
         operands.append(scale)
         specs.append(scalars)
-    operands += [*near, *far, value]
+    operands += [*[piece for piece, _ in (*near, *far)], value]
     specs += [whole] * (len(near) + len(far)) + [column]
     if before is not None:
         operands.append(before)
@@ -191,10 +193,9 @@
     return pl.pallas_call(
         functools.partial(
             absorb_kernel,
-            len(near) // 2,
             half,
-            first_near,
-            not far,
+            tuple(first for _, first in near),
+            tuple(first for _, first in far),
             before is not None,
             scale is not None,
         ),
@@ -255,7 +256,7 @@
             others = [{d: across(own[0], d) for d in near}, {}]
     own[1] = after(own[1], *others[0].values())
     own2 = jnp.stack(own)
-    cut = tall // 2
+    cut = tall * 3 // 4
 
     def is_upper(d):
         return ((row >> low_bit(d)) & 1) == 1
@@ -319,28 +320,44 @@
 
         def take_next(self, total, scale=None):
             i, d = self.left.pop(0)
-            pieces = self.found + self.partner
+            near = [(piece, 2 * i) for piece in self.found]
+            near += [(piece, at + 2 * i) for piece, at in self.partner]
             far = self.crossed[d][0] + self.crossed[d][1] if d else []
             value = flat(mixed[d] if d else own2)
-            blocks[d], *made = take(pieces, 2 * i, far, value, total, None if self.left else scale)
+            blocks[d], *made = take(near, far, value, total, None if self.left else scale)
             return made[0], made[1:]
 
         def step(self):
             self.found.append(slots.note(next_in_ring(slots.hold(self.found[-1]))))
 
-        def share(self, held=True):
-            hold = slots.hold if held else lambda value: value
-            note = slots.note if held else lambda value: value
-            for d in self.distances:
-                mine, theirs = self.crossed[d]
-                for part in mine[len(theirs) :]:
-                    theirs.append(note(other_core(hold(part))))
-            for piece in self.found[len(self.partner) :]:
-                self.partner.append(note(other_core(hold(piece))))
-                for i, d in enumerate(self.distances):
-                    part = hold(piece[2 * i : 2 * i + 2])
-                    part = jnp.where(is_upper(d), jnp.flip(part, 0), part)
-                    self.crossed[d][0].append(note(across(part, d)))
+        def swaps(self):
+            wanted = []
+            for mine, theirs in self.crossed.values():
+                wanted += [(part[at : at + 2], theirs) for part, at in mine[len(theirs) :]]
+            return wanted + [(piece, self.partner) for piece in self.found[len(self.partner) :]]
+
+        def cross(self):
+            for i, d in enumerate(self.distances):
+                mine = self.crossed[d][0]
+                parts = []
+                for piece in self.found[len(mine) :]:
+                    part = slots.hold(piece[2 * i : 2 * i + 2])
+                    parts.append(jnp.where(is_upper(d), jnp.flip(part, 0), part))
+                if parts:
+                    moved = across(jnp.concatenate(parts) if parts[1:] else parts[0], d)
+                    mine += [(slots.note(moved), 2 * k) for k in range(len(parts))]
+
+    def share(gathers, crossing=True):
+        wanted = [pair for gather in gathers for pair in gather.swaps()]
+        if wanted:
+            parts = [slots.hold(part) for part, _ in wanted]
+            swapped_parts = slots.note(other_core(jnp.concatenate(parts) if parts[1:] else parts[0]))
+            at = 0
+            for part, answers in wanted:
+                answers.append((swapped_parts, at))
+                at += part.shape[0]
+        for gather in gathers if crossing else ():
+            gather.cross()
 
     places = [(ring - k + n_ring) % n_ring for k in range(n_ring)]
     places = [(2 * place + core) * half for place in places] + [
@@ -351,18 +368,18 @@
     wide = width // 2
     aligned = half % 16 == 0 and tall % 128 == 0
 
-    def take(near, first_near, far, value, before=None, scale=None):
+    def take(near, far, value, before=None, scale=None):
         if aligned:
-            return absorb(places, near, first_near, far, value, wide, before, scale)
-
-        def tiles(pieces):
-            full = jnp.zeros((pieces[0].shape[0], tall, tall), BF16)
-            for k, piece in enumerate(pieces):
-                full = lax.dynamic_update_slice(full, piece, (0, places[k], 0))
+            return absorb(places, near, far, value, wide, before, scale)
+
+        def tiles(pieces, count):
+            full = jnp.zeros((count, tall, tall), BF16)
+            for k, (piece, at) in enumerate(pieces):
+                full = lax.dynamic_update_slice(full, piece[at : at + count], (0, places[k], 0))
             return full
 
-        near = tiles([piece[first_near : first_near + (2 if far else 3)] for piece in near])
-        b, c = tiles(far).transpose(0, 2, 1) if far else (near[2], near[2].T)
+        near = tiles(near, 2 if far else 3)
+        b, c = tiles(far, 2).transpose(0, 2, 1) if far else (near[2], near[2].T)
         block = jnp.concatenate(
             [jnp.concatenate([near[0], b], axis=1), jnp.concatenate([c, near[1]], axis=1)], axis=0
         )
@@ -403,6 +420,12 @@
 
     parts = (slice(0, cut), slice(cut, tall))
     move_second_half(parts[0])
+    sumsq = after(sumsq, own[1])
+    step = 2
+    while step < n_col:
+        sumsq = sumsq + lax.ppermute(sumsq, "col", xor_pairs(n_col, step))
+        step *= 2
+    slots.note(sumsq)
     reduces = [[Reduce([gram_term(own2, own2), gram_term(own2[:1], own2[1:])]), []]]
     slots.close()
     gathers, terms = [], {}
@@ -412,19 +435,12 @@
     while reduces or waiting or terms or any(len(g.found) < n_ring for g in gathers):
         if number == 2:
             move_second_half(parts[1])
-            step = 2
-            sumsq = slots.hold(sumsq)
-            while step < n_col:
-                sumsq = sumsq + lax.ppermute(sumsq, "col", xor_pairs(n_col, step))
-                step *= 2
-            slots.note(sumsq)
         elif number in (3, 4):
             move_to_diagonal(parts[number - 3])
-        for gather in gathers:
-            gather.share()
         stepping = [run for run, _ in reduces][:2]
-        stepping += [g for g in gathers if g.distances and len(g.found) < n_ring][: 2 - len(stepping)][:1]
+        stepping += [g for g in gathers if g.distances and len(g.found) < n_ring][: 2 - len(stepping)]
         stepping += [g for g in gathers if not g.distances and len(g.found) < n_ring]
+        share(gathers, len(stepping) <= 2)
         for run in stepping:
             run.step()
         opened = None
@@ -432,7 +448,8 @@
             for group in groups[:1]:
                 if all(d in terms for d in group):
                     opened = [Reduce([terms.pop(d) for d in group]), groups.pop(0)]
-        if waiting and number >= waiting[0][1]:
+                    opened[0].step()
+        while waiting and number >= waiting[0][1]:
             d = waiting.pop(0)[0]
             terms[d] = make_term(d)
         complete = [gather for gather in gathers if gather.complete() and not gather.taken]
@@ -449,11 +466,13 @@
     factor = rms_target * math.sqrt(m_total) / (jnp.sqrt(sumsq) + 1e-07)
     factor_sq = factor * factor
     scale = factor_sq.reshape(1)
-    for gather in gathers:
-        gather.share()
+    share(gathers)
+    for gather in gathers[:-1]:
+        if not gather.taken and gather.complete():
+            total, rounded = gather.take_next(total)
+            slots.note(total)
     slots.close()
-    for gather in gathers:
-        gather.share(False)
+    share(gathers)
     for gather in gathers:
         while not gather.taken:
             total, rounded = gather.take_next(total, scale if gather is gathers[-1] else None)
@@ -479,13 +498,17 @@
         one, two = after(found[1][0], tie), after(found[2][1], tie)
         return across(one, 2), across(two, 1)
 
-    def nearby(value, found, tie):
+    def nearby(value, found, tie, later=False):
         second = product(0, flat(after(value, tie)))
-        for d in near:
+        for d in near[:-1] if later else near:
             second = second + product(d, flat(swapped(*[after(v, tie) for v in found[d]], d)))
         return second
 
     def finish(side, second, corner, *ties):
+        if side == 0:
+            d = near[-1]
+            halves = [after(v, *ties) for v in found[0][d]]
+            second = second + product(d, flat(swapped(*halves, d)))
         if corner:
             second = second + product(3, flat(swapped(*[after(v, *ties) for v in corner], 3)))
         mine = flat(own2)[:, (left, right)[side]].astype(F32)
@@ -498,7 +521,7 @@
     found = [send(rounds[0])]
     ended = lax.optimization_barrier((rounds[1], *found[0].values()))[0]
     corner = forward(found[0], ended)
-    second = nearby(rounds[0], found[0], ended)
+    second = nearby(rounds[0], found[0], ended, True)
     ended = lax.optimization_barrier((second, *corner))[0]
     found.append(send(rounds[1], ended))
     block = finish(0, second, corner, ended)

time: 728 us -> 704 us (0.967)
  waiting for transfers between devices: 353 us -> 335 us
    ppermute x32 -> x30, waiting for transfers between devices: 126 us -> 101 us  [across(): return lax.ppermute(value, 'row', xor_pairs(n_row, distance))]
    ppermute x18, waiting for transfers between devices: 117 us -> 136 us  [next_in_ring(): return lax.ppermute(value, 'col', shift_pairs(n_col, 2))]
    ppermute x18, starting transfers between devices: 19.5 us -> 31.8 us  [next_in_ring(): return lax.ppermute(value, 'col', shift_pairs(n_col, 2))]
    ppermute x37 -> x22, starting transfers between devices: 34.8 us -> 28.5 us  [other_core(): return lax.ppermute(value, 'col', xor_pairs(n_col, 1))]
    ppermute x32 -> x30, starting transfers between devices: 31.7 us -> 28.9 us  [across(): return lax.ppermute(value, 'row', xor_pairs(n_row, distance))]
    pallas_call x5 -> x6, Pallas kernels: 58.1 us -> 57.5 us  [the longest x4 46.6 us: absorb(): pl.pallas_call(functools.partial(absorb_kernel, half, tuple((first for _,...]
  transfers between devices with their start and end apart: 93 -> 76, of which waited for: 41 -> 41; matrix products, arithmetic and copies ran while one was open for 18% -> 20% of each run, Pallas kernels for 5% -> 6%
where the time goes in v3:
time: 704 us; the launch traced here: 692 us
  waiting for transfers between devices  335 us (48%)
  starting transfers between devices  123 us (17%)
  matrix products  95.4 us (14%)
  Pallas kernels  57.5 us (8%)
  local copies, waits for them, and re-layouts  40.6 us (6%)
  other arithmetic  34.5 us (5%)
    ppermute x18, waiting for transfers between devices, next_in_ring(): return lax.ppermute(value, 'col', shift_pairs(n_col, 2))  136 us
    ppermute x30, waiting for transfers between devices, across(): return lax.ppermute(value, 'row', xor_pairs(n_row, distance))  101 us
    dot_general x12, matrix products, product(): return jnp.dot(blocks[d], value, preferred_element_type=F32)  71.8 us
    all_to_all x2, waiting for transfers between devices, shards(): block = lax.all_to_all(raw_halves[h], 'col', split_axis=0, concat_axis=0)  62.1 us
    pallas_call x4, Pallas kernels, absorb(): pl.pallas_call(functools.partial(absorb_kernel, half, tuple((first for _,...  46.6 us
    all_to_all x2, waiting for transfers between devices, send_back(): return lax.all_to_all(block, 'col', split_axis=1, concat_axis=1, tiled=True)  32.6 us
    ppermute x18, starting transfers between devices, next_in_ring(): return lax.ppermute(value, 'col', shift_pairs(n_col, 2))  31.8 us
    ppermute x30, starting transfers between devices, across(): return lax.ppermute(value, 'row', xor_pairs(n_row, distance))  28.9 us
  transfers between devices with their start and end apart: 76, of which 41 were waited for; matrix products, arithmetic and copies ran while one was open for 20% of the time, Pallas kernels for 6%

profile of v3, /device:TPU:9, one launch (start us, length us, event | category | flops | bytes accessed | tf_op | source)
XLA Modules:
  0.0 692.1 jit_solution(2303001295666069565)
XLA Ops:
  27.0 24.6 %all-to-all-done = bf16[8,112,1024]{2,1,0:T(8,128)(2,1)S(1)} async-done(((bf16[8,112,1024]{2,1,0:T(8,128)(2,1)}), bf16[8,112,1024]{2,1,0:T(8,128)(2,1)S(1)}, u32[]{:S(2)}, u32[]{:S(2)}) %all-to-all-start) | async-done | bytes 1835040 | tf_op jit(solution)/shard_map/all_to_all | solution.py:253
  62.4 37.4 %all-to-all-done.1 = bf16[8,112,1024]{2,1,0:T(8,128)(2,1)S(1)} async-done(((bf16[8,112,1024]{2,1,0:T(8,128)(2,1)}), bf16[8,112,1024]{2,1,0:T(8,128)(2,1)S(1)}, u32[]{:S(2)}, u32[]{:S(2)}) %all-to-all-start.1) | async-done | bytes 1835040 | tf_op jit(solution)/shard_map/all_to_all | solution.py:253
  168.1 10.0 %collective-permute-done.16 = bf16[672,1024]{1,0:T(8,128)(2,1)S(1)} collective-permute-done((bf16[672,1024]{1,0:T(8,128)(2,1)S(1)}, bf16[672,1024]{1,0:T(8,128)(2,1)S(1)}, u32[]{:S(2)}, u32[]{:S(2)}) %collective-permute-start.16) | collective-permute-done | bytes 1376288 | tf_op jit(solution)/shard_map/ppermute | solution.py:233
  203.7 16.9 %collective-permute-done.26 = bf16[4,112,896]{2,1,0:T(8,128)(2,1)S(1)} collective-permute-done((bf16[4,112,896]{2,1,0:T(8,128)(2,1)S(1)}, bf16[4,112,896]{2,1,0:T(8,128)(2,1)S(1)}, u32[]{:S(2)}, u32[]{:S(2)}) %collective-permute-start.26) | collective-permute-done | bytes 802848 | tf_op jit(solution)/shard_map/ppermute | solution.py:239
  235.6 17.2 %collective-permute-done.28 = bf16[4,112,896]{2,1,0:T(8,128)(2,1)S(1)} collective-permute-done((bf16[4,112,896]{2,1,0:T(8,128)(2,1)S(1)}, bf16[4,112,896]{2,1,0:T(8,128)(2,1)S(1)}, u32[]{:S(2)}, u32[]{:S(2)}) %collective-permute-start.28) | collective-permute-done | bytes 802848 | tf_op jit(solution)/shard_map/ppermute | solution.py:239
  264.1 22.8 %collective-permute-done.31 = bf16[2,112,896]{2,1,0:T(8,128)(2,1)S(1)} collective-permute-done((bf16[2,112,896]{2,1,0:T(8,128)(2,1)S(1)}, bf16[2,112,896]{2,1,0:T(8,128)(2,1)S(1)}, u32[]{:S(2)}, u32[]{:S(2)}) %collective-permute-start.31) | collective-permute-done | bytes 401440 | tf_op jit(solution)/shard_map/ppermute | solution.py:239
  288.1 11.6 %collective-permute-done.35.refs_3_ = bf16[3,112,896]{2,1,0:T(8,128)(2,1)S(1)} collective-permute-done((bf16[3,112,896]{2,1,0:T(8,128)(2,1)S(1)}, bf16[3,112,896]{2,1,0:T(8,128)(2,1)S(1)}, u32[]{:S(2)}, u32[]{:S(2)}) %collective-permute-start.35) | collective-permute-done | bytes 602144 | tf_op jit(solution)/shard_map/ppermute | solution.py:239
  307.1 24.4 %collective-permute-done.38 = bf16[2,112,896]{2,1,0:T(8,128)(2,1)S(1)} collective-permute-done((bf16[2,112,896]{2,1,0:T(8,128)(2,1)S(1)}, bf16[2,112,896]{2,1,0:T(8,128)(2,1)S(1)}, u32[]{:S(2)}, u32[]{:S(2)}) %collective-permute-start.38) | collective-permute-done | bytes 401440 | tf_op jit(solution)/shard_map/ppermute | solution.py:239
  332.5 12.0 %collective-permute-done.41.refs_4_ = bf16[3,112,896]{2,1,0:T(8,128)(2,1)S(1)} collective-permute-done((bf16[3,112,896]{2,1,0:T(8,128)(2,1)S(1)}, bf16[3,112,896]{2,1,0:T(8,128)(2,1)S(1)}, u32[]{:S(2)}, u32[]{:S(2)}) %collective-permute-start.41) | collective-permute-done | bytes 602144 | tf_op jit(solution)/shard_map/ppermute | solution.py:239
  369.7 10.9 %shard_map.43 = (bf16[1792,1792]{1,0:T(8,128)(2,1)}, f32[1792,512]{1,0:T(8,128)}) custom-call(s32[8]{0:T(128)} %stack.124.refs_0_, bf16[3,112,896]{2,1,0:T(8,128)(2,1)} %copy-done.51, bf16[3,112,896]{2,1,0:T(8,128)(2,1)} %copy-done.58, bf16[3,112,896]{2,1,0:T(8,128)(2,1)} %copy-done.52, bf16[3,112,896]{2,1,0:T(8,128)(2,1)} %copy-done.53, ...), custom_call_target="tpu_custom_call" | custom-call | flops 3288334336 | bytes 24084480 | tf_op jit(solution)/shard_map/pallas_call | solution.py:193
  398.3 9.3 %collective-permute-done.51.refs_10_ = bf16[2,112,896]{2,1,0:T(8,128)(2,1)S(1)} collective-permute-done((bf16[2,112,896]{2,1,0:T(8,128)(2,1)S(1)}, bf16[2,112,896]{2,1,0:T(8,128)(2,1)S(1)}, u32[]{:S(2)}, u32[]{:S(2)}) %collective-permute-start.51) | collective-permute-done | bytes 401440 | tf_op jit(solution)/shard_map/ppermute | solution.py:233
  425.8 9.0 %collective-permute-done.57.refs_11_ = bf16[2,112,896]{2,1,0:T(8,128)(2,1)S(1)} collective-permute-done((bf16[2,112,896]{2,1,0:T(8,128)(2,1)S(1)}, bf16[2,112,896]{2,1,0:T(8,128)(2,1)S(1)}, u32[]{:S(2)}, u32[]{:S(2)}) %collective-permute-start.57) | collective-permute-done | bytes 401440 | tf_op jit(solution)/shard_map/ppermute | solution.py:233
  444.8 11.7 %shard_map.44 = (bf16[1792,1792]{1,0:T(8,128)(2,1)}, f32[1792,512]{1,0:T(8,128)}) custom-call(s32[8]{0:T(128)} %stack.124.refs_0_, bf16[4,112,896]{2,1,0:T(8,128)(2,1)} %copy-done.3, bf16[4,112,896]{2,1,0:T(8,128)(2,1)} %copy-done.7, bf16[4,112,896]{2,1,0:T(8,128)(2,1)} %copy-done.9, bf16[4,112,896]{2,1,0:T(8,128)(2,1)} %copy-done.10, ...), custom_call_target="tpu_custom_call" | custom-call | flops 3288334336 | bytes 24084480 | tf_op jit(solution)/shard_map/pallas_call | solution.py:193
  471.4 11.6 %shard_map.45 = (bf16[1792,1792]{1,0:T(8,128)(2,1)}, f32[1792,512]{1,0:T(8,128)}) custom-call(s32[8]{0:T(128)} %stack.124.refs_0_, bf16[4,112,896]{2,1,0:T(8,128)(2,1)} %copy-done.3, bf16[4,112,896]{2,1,0:T(8,128)(2,1)} %copy-done.7, bf16[4,112,896]{2,1,0:T(8,128)(2,1)} %copy-done.9, bf16[4,112,896]{2,1,0:T(8,128)(2,1)} %copy-done.10, ...), custom_call_target="tpu_custom_call" | custom-call | flops 3288334336 | bytes 24084480 | tf_op jit(solution)/shard_map/pallas_call | solution.py:193
  484.0 12.4 %shard_map.46 = (bf16[1792,1792]{1,0:T(8,128)(2,1)}, f32[1792,512]{1,0:T(8,128)}, bf16[1792,512]{1,0:T(8,128)(2,1)}) custom-call(s32[8]{0:T(128)} %stack.124.refs_0_, f32[1]{0:T(128)} %bitcast.13.refs_1_, bf16[2,112,896]{2,1,0:T(8,128)(2,1)} %copy-done.31, bf16[2,112,896]{2,1,0:T(8,128)(2,1)} %copy-done.36, bf16[2,112,896]{2,1,0:T(8,128)(2,1)} %copy-done.30, ...), custom_call_target="tpu_custom_call" | custom-call | flops 3288334336 | bytes 24084480 | tf_op jit(solution)/shard_map/pallas_call | solution.py:193
  497.7 8.3 %fusion.4 = f32[1792,512]{1,0:T(8,128)} fusion(bf16[1792,1792]{1,0:T(8,128)(2,1)} %get-tuple-element.191, bf16[1792,1024]{1,0:T(8,128)(2,1)S(1)} %bitcast.238), kind=kOutput, calls=%fused_computation.25 | convolution fusion | flops 3288334336 | bytes 11927552 | tf_op jit(solution)/shard_map/dot_general | solution.py:481
  505.9 8.3 %fusion.6 = f32[1792,512]{1,0:T(8,128)} fusion(bf16[1792,1792]{1,0:T(8,128)(2,1)} %get-tuple-element.189, bf16[1792,1024]{1,0:T(8,128)(2,1)S(1)} %bitcast.236), kind=kOutput, calls=%fused_computation.27 | convolution fusion | flops 3288334336 | bytes 11927552 | tf_op jit(solution)/shard_map/dot_general | solution.py:481
  519.8 8.4 %fusion.20 = (bf16[1792,512]{1,0:T(8,128)(2,1)}, f32[1792,512]{1,0:T(8,128)}) fusion(f32[]{:T(128)} %bitcast.69, bf16[1792,1792]{1,0:T(8,128)(2,1)S(1)} %bitcast.289, bf16[1792,1024]{1,0:T(8,128)(2,1)S(1)} %bitcast.240, f32[1792,512]{1,0:T(8,128)} %fusion.4, f32[1792,512]{1,0:T(8,128)} %fusion.8, f32[1792,512]{1,0:T(8,128)} %fusion.6), kind=kOutput, calls=%fused_computation.177 | convolution fusion | flops 3292921856 | bytes 24772612 | tf_op jit(solution)/shard_map/dot_general | solution.py:481
  528.2 10.2 %collective-permute-done.65 = bf16[2,896,512]{2,1,0:T(8,128)(2,1)S(1)} collective-permute-done((bf16[2,896,512]{2,1,0:T(8,128)(2,1)}, bf16[2,896,512]{2,1,0:T(8,128)(2,1)S(1)}, u32[]{:S(2)}, u32[]{:S(2)}) %collective-permute-start.65) | collective-permute-done | bytes 1835040 | tf_op jit(solution)/shard_map/ppermute | solution.py:233
  551.9 7.7 %collective-permute-done.66 = bf16[896,512]{1,0:T(8,128)(2,1)S(1)} collective-permute-done((bf16[896,512]{1,0:T(8,128)(2,1)S(1)}, bf16[896,512]{1,0:T(8,128)(2,1)S(1)}, u32[]{:S(2)}, u32[]{:S(2)}) %collective-permute-start.66) | collective-permute-done | bytes 917536 | tf_op jit(solution)/shard_map/ppermute | solution.py:233
  581.0 19.1 %collective-permute-done.69 = bf16[2,896,512]{2,1,0:T(8,128)(2,1)} collective-permute-done((bf16[2,896,512]{2,1,0:T(8,128)(2,1)}, bf16[2,896,512]{2,1,0:T(8,128)(2,1)}, u32[]{:S(2)}, u32[]{:S(2)}) %collective-permute-start.69) | collective-permute-done | bytes 1835040 | tf_op jit(solution)/shard_map/ppermute | solution.py:233
  626.1 7.7 %multiply_convert_fusion = bf16[1792,512]{1,0:T(8,128)(2,1)S(1)} fusion(f32[1792,512]{1,0:T(8,128)} %add_add_fusion, f32[1792,512]{1,0:T(8,128)S(1)} %copy-done.61, bf16[1792,1792]{1,0:T(8,128)(2,1)} %get-tuple-element.193, bf16[1792,512]{1,0:T(8,128)(2,1)S(1)} %bitcast.260, bf16[1792,1024]{1,0:T(8,128)(2,1)S(1)} %bitcast.252, f32[]{:T(128)} %bitcast.85, ...), kind=kOutput, calls=%fused_computation.4 | convolution fusion | flops 3297509376 | bytes 19267592 | tf_op jit(solution)/shard_map/dot_general | solution.py:481
  635.2 9.2 %all-to-all-start.3 = ((bf16[2,8,112,512]{3,2,0,1:T(8,128)(2,1)}), bf16[2,8,112,512]{3,2,0,1:T(8,128)(2,1)}, u32[]{:S(2)}, u32[]{:S(2)}) async-start(bf16[2,8,112,512]{3,2,0,1:T(8,128)(2,1)} %copy.86), calls=%async_computation.3 | async-start | bytes 3670016 | tf_op jit(solution)/shard_map/all_to_all | solution.py:519
  651.7 32.6 %all-to-all-done.3 = bf16[2,8,112,512]{3,2,0,1:T(8,128)(2,1)} async-done(((bf16[2,8,112,512]{3,2,0,1:T(8,128)(2,1)}), bf16[2,8,112,512]{3,2,0,1:T(8,128)(2,1)}, u32[]{:S(2)}, u32[]{:S(2)}) %all-to-all-start.3) | async-done | bytes 1835040 | tf_op jit(solution)/shard_map/all_to_all | solution.py:519
  (424 shorter events, 332.0 us)
Async XLA Ops:
  6.1 45.5 %all-to-all-start = ((bf16[8,112,1024]{2,1,0:T(8,128)(2,1)}), bf16[8,112,1024]{2,1,0:T(8,128)(2,1)S(1)}, u32[]{:S(2)}, u32[]{:S(2)}) async-start(bf16[8,112,1024]{2,1,0:T(8,128)(2,1)} %get-tuple-element.109), calls=%async_computation | async-start | bytes 3670016 | tf_op jit(solution)/shard_map/all_to_all | solution.py:253
  52.8 46.9 %all-to-all-start.1 = ((bf16[8,112,1024]{2,1,0:T(8,128)(2,1)}), bf16[8,112,1024]{2,1,0:T(8,128)(2,1)S(1)}, u32[]{:S(2)}, u32[]{:S(2)}) async-start(bf16[8,112,1024]{2,1,0:T(8,128)(2,1)} %get-tuple-element.114), calls=%async_computation.1 | async-start | bytes 3670016 | tf_op jit(solution)/shard_map/all_to_all | solution.py:253
  59.9 41.6 %collective-permute-start.4 = (bf16[896,1024]{1,0:T(8,128)(2,1)}, bf16[896,1024]{1,0:T(8,128)(2,1)}, u32[]{:S(2)}, u32[]{:S(2)}) collective-permute-start(bf16[896,1024]{1,0:T(8,128)(2,1)} %bitcast.241), channel_id=1, source_target_pairs={{0,16},{8,24},{16,0},{24,8},{1,17},{9,25},{17,1},{25,9},{2,18},{10... | collective-permute-start | bytes 5505032 | tf_op jit(solution)/shard_map/ppermute | solution.py:233
  61.1 41.2 %collective-permute-start.3 = (bf16[896,1024]{1,0:T(8,128)(2,1)}, bf16[896,1024]{1,0:T(8,128)(2,1)}, u32[]{:S(2)}, u32[]{:S(2)}) collective-permute-start(bf16[896,1024]{1,0:T(8,128)(2,1)} %bitcast.242), channel_id=1, source_target_pairs={{0,8},{8,0},{16,24},{24,16},{1,9},{9,1},{17,25},{25,17},{2,10},{10... | collective-permute-start | bytes 5505032 | tf_op jit(solution)/shard_map/ppermute | solution.py:233
  102.5 30.2 %collective-permute-start.8 = (bf16[672,1024]{1,0:T(8,128)(2,1)S(1)}, bf16[672,1024]{1,0:T(8,128)(2,1)S(1)}, u32[]{:S(2)}, u32[]{:S(2)}) collective-permute-start(bf16[672,1024]{1,0:T(8,128)(2,1)S(1)} %slice.121), channel_id=1, source_target_pairs={{0,8},{8,0},{16,24},{24,16},{1,9},{9,1},{17,25},{25,17},{2,10},{10... | collective-permute-start | bytes 4128776 | tf_op jit(solution)/shard_map/ppermute | solution.py:233
  103.8 29.9 %collective-permute-start.7 = (bf16[672,1024]{1,0:T(8,128)(2,1)S(1)}, bf16[672,1024]{1,0:T(8,128)(2,1)S(1)}, u32[]{:S(2)}, u32[]{:S(2)}) collective-permute-start(bf16[672,1024]{1,0:T(8,128)(2,1)S(1)} %slice.121), channel_id=1, source_target_pairs={{0,16},{8,24},{16,0},{24,8},{1,17},{9,25},{17,1},{25,9},{2,18},{10... | collective-permute-start | bytes 4128776 | tf_op jit(solution)/shard_map/ppermute | solution.py:233
  142.2 45.0 %collective-permute-start.11 = (bf16[3,112,896]{2,1,0:T(8,128)(2,1)S(1)}, bf16[3,112,896]{2,1,0:T(8,128)(2,1)S(1)}, u32[]{:S(2)}, u32[]{:S(2)}) collective-permute-start(bf16[3,112,896]{2,1,0:T(8,128)(2,1)S(1)} %pad_maximum_fusion.26), channel_id=1, source_target_pairs={{0,1},{1,0},{2,3},{3,2},{4,5},{5,4},{6,7},{7,6},{8,9},{9,8},{10,11... | collective-permute-start | bytes 1806344 | tf_op jit(solution)/shard_map/ppermute | solution.py:236
  189.9 30.8 %collective-permute-start.26 = (bf16[4,112,896]{2,1,0:T(8,128)(2,1)S(1)}, bf16[4,112,896]{2,1,0:T(8,128)(2,1)S(1)}, u32[]{:S(2)}, u32[]{:S(2)}) collective-permute-start(bf16[4,112,896]{2,1,0:T(8,128)(2,1)S(1)} %fusion.11), channel_id=1, source_target_pairs={{0,2},{1,3},{2,4},{3,5},{4,6},{5,7},{6,0},{7,1},{8,10},{9,11},{10,... | collective-permute-start | bytes 2408456 | tf_op jit(solution)/shard_map/ppermute | solution.py:239
  200.2 56.1 %collective-permute-start.24 = (bf16[4,112,896]{2,1,0:T(8,128)(2,1)S(1)}, bf16[4,112,896]{2,1,0:T(8,128)(2,1)S(1)}, u32[]{:S(2)}, u32[]{:S(2)}) collective-permute-start(bf16[4,112,896]{2,1,0:T(8,128)(2,1)S(1)} %pad_maximum_fusion.19), channel_id=1, source_target_pairs={{0,1},{1,0},{2,3},{3,2},{4,5},{5,4},{6,7},{7,6},{8,9},{9,8},{10,11... | collective-permute-start | bytes 2408456 | tf_op jit(solution)/shard_map/ppermute | solution.py:236
  255.7 44.1 %collective-permute-start.25 = (bf16[4,112,896]{2,1,0:T(8,128)(2,1)S(1)}, bf16[4,112,896]{2,1,0:T(8,128)(2,1)S(1)}, u32[]{:S(2)}, u32[]{:S(2)}) collective-permute-start(bf16[4,112,896]{2,1,0:T(8,128)(2,1)S(1)} %pad_maximum_fusion.20), channel_id=1, source_target_pairs={{0,1},{1,0},{2,3},{3,2},{4,5},{5,4},{6,7},{7,6},{8,9},{9,8},{10,11... | collective-permute-start | bytes 2408456 | tf_op jit(solution)/shard_map/ppermute | solution.py:236
  256.6 43.2 %collective-permute-start.34 = (bf16[4,112,896]{2,1,0:T(8,128)(2,1)S(1)}, bf16[4,112,896]{2,1,0:T(8,128)(2,1)S(1)}, u32[]{:S(2)}, u32[]{:S(2)}) collective-permute-start(bf16[4,112,896]{2,1,0:T(8,128)(2,1)S(1)} %add_convert_fusion.1), channel_id=1, source_target_pairs={{0,2},{1,3},{2,4},{3,5},{4,6},{5,7},{6,0},{7,1},{8,10},{9,11},{10,... | collective-permute-start | bytes 2408456 | tf_op jit(solution)/shard_map/ppermute | solution.py:239
  259.5 40.3 %collective-permute-start.35 = (bf16[3,112,896]{2,1,0:T(8,128)(2,1)S(1)}, bf16[3,112,896]{2,1,0:T(8,128)(2,1)S(1)}, u32[]{:S(2)}, u32[]{:S(2)}) collective-permute-start(bf16[3,112,896]{2,1,0:T(8,128)(2,1)S(1)} %collective-permute-done.29.refs_2_), channel_id=1, source_target_pairs={{0,2},{1,3},{2,4},{3,5},{4,6},{5,7},{6,0},{7,1},{8,10},{9,11},{10,... | collective-permute-start | bytes 1806344 | tf_op jit(solution)/shard_map/ppermute | solution.py:239
  263.2 36.6 %collective-permute-start.33 = (bf16[3,112,896]{2,1,0:T(8,128)(2,1)S(1)}, bf16[3,112,896]{2,1,0:T(8,128)(2,1)S(1)}, u32[]{:S(2)}, u32[]{:S(2)}) collective-permute-start(bf16[3,112,896]{2,1,0:T(8,128)(2,1)S(1)} %collective-permute-done.29.refs_2_), channel_id=1, source_target_pairs={{0,1},{1,0},{2,3},{3,2},{4,5},{5,4},{6,7},{7,6},{8,9},{9,8},{10,11... | collective-permute-start | bytes 1806344 | tf_op jit(solution)/shard_map/ppermute | solution.py:236
  300.7 43.7 %collective-permute-start.39 = (bf16[7,112,896]{2,1,0:T(8,128)(2,1)S(1)}, bf16[7,112,896]{2,1,0:T(8,128)(2,1)}, u32[]{:S(2)}, u32[]{:S(2)}) collective-permute-start(bf16[7,112,896]{2,1,0:T(8,128)(2,1)S(1)} %pad_maximum_fusion.15), channel_id=1, source_target_pairs={{0,1},{1,0},{2,3},{3,2},{4,5},{5,4},{6,7},{7,6},{8,9},{9,8},{10,11... | collective-permute-start | bytes 4214792 | tf_op jit(solution)/shard_map/ppermute | solution.py:236
  301.4 31.0 %collective-permute-start.40 = (bf16[4,112,896]{2,1,0:T(8,128)(2,1)S(1)}, bf16[4,112,896]{2,1,0:T(8,128)(2,1)S(1)}, u32[]{:S(2)}, u32[]{:S(2)}) collective-permute-start(bf16[4,112,896]{2,1,0:T(8,128)(2,1)S(1)} %add_convert_fusion.refs_1_), channel_id=1, source_target_pairs={{0,2},{1,3},{2,4},{3,5},{4,6},{5,7},{6,0},{7,1},{8,10},{9,11},{10,... | collective-permute-start | bytes 2408456 | tf_op jit(solution)/shard_map/ppermute | solution.py:239
  301.4 30.1 %collective-permute-start.38 = (bf16[2,112,896]{2,1,0:T(8,128)(2,1)S(1)}, bf16[2,112,896]{2,1,0:T(8,128)(2,1)S(1)}, u32[]{:S(2)}, u32[]{:S(2)}) collective-permute-start(bf16[2,112,896]{2,1,0:T(8,128)(2,1)S(1)} %get-tuple-element.146), channel_id=1, source_target_pairs={{0,2},{1,3},{2,4},{3,5},{4,6},{5,7},{6,0},{7,1},{8,10},{9,11},{10,... | collective-permute-start | bytes 1204232 | tf_op jit(solution)/shard_map/ppermute | solution.py:239
  303.0 41.4 %collective-permute-start.41 = (bf16[3,112,896]{2,1,0:T(8,128)(2,1)S(1)}, bf16[3,112,896]{2,1,0:T(8,128)(2,1)S(1)}, u32[]{:S(2)}, u32[]{:S(2)}) collective-permute-start(bf16[3,112,896]{2,1,0:T(8,128)(2,1)S(1)} %collective-permute-done.35.refs_3_), channel_id=1, source_target_pairs={{0,2},{1,3},{2,4},{3,5},{4,6},{5,7},{6,0},{7,1},{8,10},{9,11},{10,... | collective-permute-start | bytes 1806344 | tf_op jit(solution)/shard_map/ppermute | solution.py:239
  381.0 31.1 %collective-permute-start.48 = (bf16[14,112,896]{2,1,0:T(8,128)(2,1)S(1)}, bf16[14,112,896]{2,1,0:T(8,128)(2,1)S(1)}, u32[]{:S(2)}, u32[]{:S(2)}) collective-permute-start(bf16[14,112,896]{2,1,0:T(8,128)(2,1)S(1)} %get-tuple-element.313), channel_id=1, source_target_pairs={{0,1},{1,0},{2,3},{3,2},{4,5},{5,4},{6,7},{7,6},{8,9},{9,8},{10,11... | collective-permute-start | bytes 8429576 | tf_op jit(solution)/shard_map/ppermute | solution.py:236
  496.4 41.9 %collective-permute-start.65 = (bf16[2,896,512]{2,1,0:T(8,128)(2,1)}, bf16[2,896,512]{2,1,0:T(8,128)(2,1)S(1)}, u32[]{:S(2)}, u32[]{:S(2)}) collective-permute-start(bf16[2,896,512]{2,1,0:T(8,128)(2,1)} %bitcast.294), channel_id=1, source_target_pairs={{0,16},{8,24},{16,0},{24,8},{1,17},{9,25},{17,1},{25,9},{2,18},{10... | collective-permute-start | bytes 5505032 | tf_op jit(solution)/shard_map/ppermute | solution.py:233
  496.7 41.7 %collective-permute-start.64 = (bf16[2,896,512]{2,1,0:T(8,128)(2,1)}, bf16[2,896,512]{2,1,0:T(8,128)(2,1)S(1)}, u32[]{:S(2)}, u32[]{:S(2)}) collective-permute-start(bf16[2,896,512]{2,1,0:T(8,128)(2,1)} %bitcast.295), channel_id=1, source_target_pairs={{0,8},{8,0},{16,24},{24,16},{1,9},{9,1},{17,25},{25,17},{2,10},{10... | collective-permute-start | bytes 5505032 | tf_op jit(solution)/shard_map/ppermute | solution.py:233
  560.6 39.5 %collective-permute-start.69 = (bf16[2,896,512]{2,1,0:T(8,128)(2,1)}, bf16[2,896,512]{2,1,0:T(8,128)(2,1)}, u32[]{:S(2)}, u32[]{:S(2)}) collective-permute-start(bf16[2,896,512]{2,1,0:T(8,128)(2,1)} %bitcast.70), channel_id=1, source_target_pairs={{0,16},{8,24},{16,0},{24,8},{1,17},{9,25},{17,1},{25,9},{2,18},{10... | collective-permute-start | bytes 5505032 | tf_op jit(solution)/shard_map/ppermute | solution.py:233
  561.0 39.4 %collective-permute-start.68 = (bf16[2,896,512]{2,1,0:T(8,128)(2,1)}, bf16[2,896,512]{2,1,0:T(8,128)(2,1)}, u32[]{:S(2)}, u32[]{:S(2)}) collective-permute-start(bf16[2,896,512]{2,1,0:T(8,128)(2,1)} %bitcast.70), channel_id=1, source_target_pairs={{0,8},{8,0},{16,24},{24,16},{1,9},{9,1},{17,25},{25,17},{2,10},{10... | collective-permute-start | bytes 5505032 | tf_op jit(solution)/shard_map/ppermute | solution.py:233
  573.7 49.0 %all-to-all-start.2 = ((bf16[2,8,112,512]{3,2,0,1:T(8,128)(2,1)}), bf16[2,8,112,512]{3,2,0,1:T(8,128)(2,1)S(1)}, u32[]{:S(2)}, u32[]{:S(2)}) async-start(bf16[2,8,112,512]{3,2,0,1:T(8,128)(2,1)} %copy.85), calls=%async_computation.2 | async-start | bytes 3670016 | tf_op jit(solution)/shard_map/all_to_all | solution.py:519
  635.2 49.1 %all-to-all-start.3 = ((bf16[2,8,112,512]{3,2,0,1:T(8,128)(2,1)}), bf16[2,8,112,512]{3,2,0,1:T(8,128)(2,1)}, u32[]{:S(2)}, u32[]{:S(2)}) async-start(bf16[2,8,112,512]{3,2,0,1:T(8,128)(2,1)} %copy.86), calls=%async_computation.3 | async-start | bytes 3670016 | tf_op jit(solution)/shard_map/all_to_all | solution.py:519
  (130 other events, 1467.0 us)

commit v4 on v3

--- a/solution.py
+++ b/solution.py
@@ -256,7 +256,7 @@
             others = [{d: across(own[0], d) for d in near}, {}]
     own[1] = after(own[1], *others[0].values())
     own2 = jnp.stack(own)
-    cut = tall * 3 // 4
+    cut = tall // 2
 
     def is_upper(d):
         return ((row >> low_bit(d)) & 1) == 1
@@ -530,12 +530,20 @@
     corner = forward(found[1], ended)
     second = nearby(rounds[1], found[1], ended)
     ended = lax.optimization_barrier((second, backs[0], *corner))[0]
-    backs.append(send_back(finish(1, second, corner, ended)))
+    block = finish(1, second, corner, ended)
     update = jnp.zeros((rows, n_in), BF16)
     for side, back in enumerate(backs):
         for source in range(n_col):
             piece = back[:, source].reshape(rows, wide)
             update = lax.dynamic_update_slice(update, piece, (0, source * width + side * wide))
+    for k in range(n_col):
+        piece = lax.dynamic_index_in_dim(block, (col + k) % n_col, 1, keepdims=False)
+        if k:
+            piece = lax.ppermute(piece, "col", shift_pairs(n_col, k))
+        source = (col - k + n_col) % n_col
+        update = lax.dynamic_update_slice(
+            update, piece.reshape(rows, -1), (0, source * width + wide)
+        )
     return (update, new_momentum)
 
 

time: 704 us -> 693 us (0.984)
  local copies, waits for them, and re-layouts: 40.6 us -> 26.5 us
    ppermute x0 -> x7, waiting for transfers between devices: none -> 34.4 us  [shards(): piece = lax.ppermute(piece, 'col', shift_pairs(n_col, k))]
    all_to_all x2 -> x1, waiting for transfers between devices: 32.6 us -> 0.63 us  [send_back(): return lax.all_to_all(block, 'col', split_axis=1, concat_axis=1, tiled=True)]
    ppermute x30, waiting for transfers between devices: 101 us -> 85.5 us  [across(): return lax.ppermute(value, 'row', xor_pairs(n_row, distance))]
    ppermute x18, waiting for transfers between devices: 136 us -> 151 us  [next_in_ring(): return lax.ppermute(value, 'col', shift_pairs(n_col, 2))]
    dynamic_update_slice x16 -> x8, local copies, waits for them, and re-layouts: 12.8 us -> 0.56 us  [shards(): lax.dynamic_update_slice(update, piece, (0, source * width + side * wide))]
    ppermute x0 -> x7, starting transfers between devices: none -> 10.7 us  [shards(): piece = lax.ppermute(piece, 'col', shift_pairs(n_col, k))]
    all_to_all x2 -> x1, starting transfers between devices: 16.5 us -> 7.62 us  [send_back(): return lax.all_to_all(block, 'col', split_axis=1, concat_axis=1, tiled=True)]
  transfers between devices with their start and end apart: 76 -> 82, of which waited for: 41 -> 45; matrix products, arithmetic and copies ran while one was open for 20% -> 20% of each run, Pallas kernels for 6% -> 6%
where the time goes in v4:
time: 693 us; the launch traced here: 685 us
  waiting for transfers between devices  336 us (48%)
  starting transfers between devices  125 us (18%)
  matrix products  96.6 us (14%)
  Pallas kernels  57.4 us (8%)
  other arithmetic  37.4 us (5%)
  local copies, waits for them, and re-layouts  26.5 us (4%)
    ppermute x18, waiting for transfers between devices, next_in_ring(): return lax.ppermute(value, 'col', shift_pairs(n_col, 2))  151 us
    ppermute x30, waiting for transfers between devices, across(): return lax.ppermute(value, 'row', xor_pairs(n_row, distance))  85.5 us
    dot_general x12, matrix products, product(): return jnp.dot(blocks[d], value, preferred_element_type=F32)  74.4 us
    all_to_all x2, waiting for transfers between devices, shards(): block = lax.all_to_all(raw_halves[h], 'col', split_axis=0, concat_axis=0)  62.2 us
    pallas_call x4, Pallas kernels, absorb(): pl.pallas_call(functools.partial(absorb_kernel, half, tuple((first for _,...  46.4 us
    ppermute x7, waiting for transfers between devices, shards(): piece = lax.ppermute(piece, 'col', shift_pairs(n_col, k))  34.4 us
    ppermute x30, starting transfers between devices, across(): return lax.ppermute(value, 'row', xor_pairs(n_row, distance))  31.3 us
    ppermute x22, starting transfers between devices, other_core(): return lax.ppermute(value, 'col', xor_pairs(n_col, 1))  31 us
  transfers between devices with their start and end apart: 82, of which 45 were waited for; matrix products, arithmetic and copies ran while one was open for 20% of the time, Pallas kernels for 6%

profile of v4, /device:TPU:9, one launch (start us, length us, event | category | flops | bytes accessed | tf_op | source)
XLA Modules:
  0.0 685.2 jit_solution(12802573114568140885)
XLA Ops:
  26.9 24.7 %all-to-all-done = bf16[8,112,1024]{2,1,0:T(8,128)(2,1)S(1)} async-done(((bf16[8,112,1024]{2,1,0:T(8,128)(2,1)}), bf16[8,112,1024]{2,1,0:T(8,128)(2,1)S(1)}, u32[]{:S(2)}, u32[]{:S(2)}) %all-to-all-start) | async-done | bytes 1835040 | tf_op jit(solution)/shard_map/all_to_all | solution.py:253
  62.4 37.4 %all-to-all-done.1 = bf16[8,112,1024]{2,1,0:T(8,128)(2,1)S(1)} async-done(((bf16[8,112,1024]{2,1,0:T(8,128)(2,1)}), bf16[8,112,1024]{2,1,0:T(8,128)(2,1)S(1)}, u32[]{:S(2)}, u32[]{:S(2)}) %all-to-all-start.1) | async-done | bytes 1835040 | tf_op jit(solution)/shard_map/all_to_all | solution.py:253
  177.7 10.5 %collective-permute-done.21 = bf16[3,112,896]{2,1,0:T(8,128)(2,1)S(1)} collective-permute-done((bf16[3,112,896]{2,1,0:T(8,128)(2,1)S(1)}, bf16[3,112,896]{2,1,0:T(8,128)(2,1)S(1)}, u32[]{:S(2)}, u32[]{:S(2)}) %collective-permute-start.21) | collective-permute-done | bytes 602144 | tf_op jit(solution)/shard_map/ppermute | solution.py:239
  194.5 11.0 %collective-permute-done.26 = bf16[4,112,896]{2,1,0:T(8,128)(2,1)S(1)} collective-permute-done((bf16[4,112,896]{2,1,0:T(8,128)(2,1)S(1)}, bf16[4,112,896]{2,1,0:T(8,128)(2,1)S(1)}, u32[]{:S(2)}, u32[]{:S(2)}) %collective-permute-start.26) | collective-permute-done | bytes 802848 | tf_op jit(solution)/shard_map/ppermute | solution.py:239
  214.6 8.7 %collective-permute-done.29.refs_2_ = bf16[3,112,896]{2,1,0:T(8,128)(2,1)S(1)} collective-permute-done((bf16[3,112,896]{2,1,0:T(8,128)(2,1)S(1)}, bf16[3,112,896]{2,1,0:T(8,128)(2,1)S(1)}, u32[]{:S(2)}, u32[]{:S(2)}) %collective-permute-start.29) | collective-permute-done | bytes 602144 | tf_op jit(solution)/shard_map/ppermute | solution.py:239
  223.2 17.2 %collective-permute-done.28 = bf16[4,112,896]{2,1,0:T(8,128)(2,1)S(1)} collective-permute-done((bf16[4,112,896]{2,1,0:T(8,128)(2,1)S(1)}, bf16[4,112,896]{2,1,0:T(8,128)(2,1)S(1)}, u32[]{:S(2)}, u32[]{:S(2)}) %collective-permute-start.28) | collective-permute-done | bytes 802848 | tf_op jit(solution)/shard_map/ppermute | solution.py:239
  249.4 23.1 %collective-permute-done.31 = bf16[2,112,896]{2,1,0:T(8,128)(2,1)S(1)} collective-permute-done((bf16[2,112,896]{2,1,0:T(8,128)(2,1)S(1)}, bf16[2,112,896]{2,1,0:T(8,128)(2,1)S(1)}, u32[]{:S(2)}, u32[]{:S(2)}) %collective-permute-start.31) | collective-permute-done | bytes 401440 | tf_op jit(solution)/shard_map/ppermute | solution.py:239
  273.8 11.6 %collective-permute-done.35.refs_3_ = bf16[3,112,896]{2,1,0:T(8,128)(2,1)S(1)} collective-permute-done((bf16[3,112,896]{2,1,0:T(8,128)(2,1)S(1)}, bf16[3,112,896]{2,1,0:T(8,128)(2,1)S(1)}, u32[]{:S(2)}, u32[]{:S(2)}) %collective-permute-start.35) | collective-permute-done | bytes 602144 | tf_op jit(solution)/shard_map/ppermute | solution.py:239
  292.4 24.3 %collective-permute-done.38 = bf16[2,112,896]{2,1,0:T(8,128)(2,1)S(1)} collective-permute-done((bf16[2,112,896]{2,1,0:T(8,128)(2,1)S(1)}, bf16[2,112,896]{2,1,0:T(8,128)(2,1)S(1)}, u32[]{:S(2)}, u32[]{:S(2)}) %collective-permute-start.38) | collective-permute-done | bytes 401440 | tf_op jit(solution)/shard_map/ppermute | solution.py:239
  317.7 11.9 %collective-permute-done.41.refs_4_ = bf16[3,112,896]{2,1,0:T(8,128)(2,1)S(1)} collective-permute-done((bf16[3,112,896]{2,1,0:T(8,128)(2,1)S(1)}, bf16[3,112,896]{2,1,0:T(8,128)(2,1)S(1)}, u32[]{:S(2)}, u32[]{:S(2)}) %collective-permute-start.41) | collective-permute-done | bytes 602144 | tf_op jit(solution)/shard_map/ppermute | solution.py:239
  354.2 10.9 %shard_map.43 = (bf16[1792,1792]{1,0:T(8,128)(2,1)}, f32[1792,512]{1,0:T(8,128)}) custom-call(s32[8]{0:T(128)} %stack.124.refs_0_, bf16[3,112,896]{2,1,0:T(8,128)(2,1)} %copy-done.50, bf16[3,112,896]{2,1,0:T(8,128)(2,1)} %copy-done.57, bf16[3,112,896]{2,1,0:T(8,128)(2,1)} %copy-done.51, bf16[3,112,896]{2,1,0:T(8,128)(2,1)} %copy-done.52, ...), custom_call_target="tpu_custom_call" | custom-call | flops 3288334336 | bytes 24084480 | tf_op jit(solution)/shard_map/pallas_call | solution.py:193
  374.7 22.2 %collective-permute-done.47.refs_3_ = bf16[2,112,896]{2,1,0:T(8,128)(2,1)S(1)} collective-permute-done((bf16[2,112,896]{2,1,0:T(8,128)(2,1)S(1)}, bf16[2,112,896]{2,1,0:T(8,128)(2,1)S(1)}, u32[]{:S(2)}, u32[]{:S(2)}) %collective-permute-start.47) | collective-permute-done | bytes 401440 | tf_op jit(solution)/shard_map/ppermute | solution.py:239
  398.5 9.3 %collective-permute-done.51.refs_10_ = bf16[2,112,896]{2,1,0:T(8,128)(2,1)S(1)} collective-permute-done((bf16[2,112,896]{2,1,0:T(8,128)(2,1)S(1)}, bf16[2,112,896]{2,1,0:T(8,128)(2,1)S(1)}, u32[]{:S(2)}, u32[]{:S(2)}) %collective-permute-start.51) | collective-permute-done | bytes 401440 | tf_op jit(solution)/shard_map/ppermute | solution.py:233
  421.4 8.6 %collective-permute-done.57.refs_11_ = bf16[2,112,896]{2,1,0:T(8,128)(2,1)S(1)} collective-permute-done((bf16[2,112,896]{2,1,0:T(8,128)(2,1)S(1)}, bf16[2,112,896]{2,1,0:T(8,128)(2,1)S(1)}, u32[]{:S(2)}, u32[]{:S(2)}) %collective-permute-start.57) | collective-permute-done | bytes 401440 | tf_op jit(solution)/shard_map/ppermute | solution.py:233
  440.5 11.6 %shard_map.44 = (bf16[1792,1792]{1,0:T(8,128)(2,1)}, f32[1792,512]{1,0:T(8,128)}) custom-call(s32[8]{0:T(128)} %stack.124.refs_0_, bf16[4,112,896]{2,1,0:T(8,128)(2,1)} %copy-done.3, bf16[4,112,896]{2,1,0:T(8,128)(2,1)} %copy-done.7, bf16[4,112,896]{2,1,0:T(8,128)(2,1)} %copy-done.8, bf16[4,112,896]{2,1,0:T(8,128)(2,1)} %copy-done.9, ...), custom_call_target="tpu_custom_call" | custom-call | flops 3288334336 | bytes 24084480 | tf_op jit(solution)/shard_map/pallas_call | solution.py:193
  467.1 11.5 %shard_map.45 = (bf16[1792,1792]{1,0:T(8,128)(2,1)}, f32[1792,512]{1,0:T(8,128)}) custom-call(s32[8]{0:T(128)} %stack.124.refs_0_, bf16[4,112,896]{2,1,0:T(8,128)(2,1)} %copy-done.3, bf16[4,112,896]{2,1,0:T(8,128)(2,1)} %copy-done.7, bf16[4,112,896]{2,1,0:T(8,128)(2,1)} %copy-done.8, bf16[4,112,896]{2,1,0:T(8,128)(2,1)} %copy-done.9, ...), custom_call_target="tpu_custom_call" | custom-call | flops 3288334336 | bytes 24084480 | tf_op jit(solution)/shard_map/pallas_call | solution.py:193
  479.7 12.4 %shard_map.46 = (bf16[1792,1792]{1,0:T(8,128)(2,1)}, f32[1792,512]{1,0:T(8,128)}, bf16[1792,512]{1,0:T(8,128)(2,1)}) custom-call(s32[8]{0:T(128)} %stack.124.refs_0_, f32[1]{0:T(128)} %bitcast.13.refs_1_, bf16[2,112,896]{2,1,0:T(8,128)(2,1)} %copy-done.29, bf16[2,112,896]{2,1,0:T(8,128)(2,1)} %copy-done.34, bf16[2,112,896]{2,1,0:T(8,128)(2,1)} %copy-done.28, ...), custom_call_target="tpu_custom_call" | custom-call | flops 3288334336 | bytes 24084480 | tf_op jit(solution)/shard_map/pallas_call | solution.py:193
  493.5 8.3 %fusion.4 = f32[1792,512]{1,0:T(8,128)} fusion(bf16[1792,1792]{1,0:T(8,128)(2,1)} %get-tuple-element.191, bf16[1792,1024]{1,0:T(8,128)(2,1)S(1)} %bitcast.251), kind=kOutput, calls=%fused_computation.25 | convolution fusion | flops 3288334336 | bytes 11927552 | tf_op jit(solution)/shard_map/dot_general | solution.py:481
  501.8 8.3 %fusion.8 = f32[1792,512]{1,0:T(8,128)} fusion(bf16[1792,1792]{1,0:T(8,128)(2,1)} %get-tuple-element.186, bf16[1792,1024]{1,0:T(8,128)(2,1)S(1)} %bitcast.263), kind=kOutput, calls=%fused_computation.29 | convolution fusion | flops 3288334336 | bytes 11927552 | tf_op jit(solution)/shard_map/dot_general | solution.py:481
  515.5 8.2 %fusion.21 = (bf16[1792,512]{1,0:T(8,128)(2,1)}, f32[1792,512]{1,0:T(8,128)}) fusion(f32[]{:T(128)} %bitcast.69, bf16[1792,1792]{1,0:T(8,128)(2,1)S(1)} %bitcast.302, bf16[1792,1024]{1,0:T(8,128)(2,1)S(1)} %bitcast.253, f32[1792,512]{1,0:T(8,128)} %fusion.4, f32[1792,512]{1,0:T(8,128)} %fusion.8, f32[1792,512]{1,0:T(8,128)} %fusion.6), kind=kOutput, calls=%fused_computation.186 | convolution fusion | flops 3292921856 | bytes 24772612 | tf_op jit(solution)/shard_map/dot_general | solution.py:481
  523.7 10.4 %collective-permute-done.64 = bf16[2,896,512]{2,1,0:T(8,128)(2,1)S(1)} collective-permute-done((bf16[2,896,512]{2,1,0:T(8,128)(2,1)}, bf16[2,896,512]{2,1,0:T(8,128)(2,1)S(1)}, u32[]{:S(2)}, u32[]{:S(2)}) %collective-permute-start.64) | collective-permute-done | bytes 1835040 | tf_op jit(solution)/shard_map/ppermute | solution.py:233
  547.7 8.0 %collective-permute-done.66 = bf16[896,512]{1,0:T(8,128)(2,1)S(1)} collective-permute-done((bf16[896,512]{1,0:T(8,128)(2,1)S(1)}, bf16[896,512]{1,0:T(8,128)(2,1)S(1)}, u32[]{:S(2)}, u32[]{:S(2)}) %collective-permute-start.66) | collective-permute-done | bytes 917536 | tf_op jit(solution)/shard_map/ppermute | solution.py:233
  585.9 15.3 %collective-permute-done.68 = bf16[2,896,512]{2,1,0:T(8,128)(2,1)} collective-permute-done((bf16[2,896,512]{2,1,0:T(8,128)(2,1)}, bf16[2,896,512]{2,1,0:T(8,128)(2,1)}, u32[]{:S(2)}, u32[]{:S(2)}) %collective-permute-start.68) | collective-permute-done | bytes 1835040 | tf_op jit(solution)/shard_map/ppermute | solution.py:233
  652.7 24.4 %collective-permute-done.74 = bf16[2,112,512]{2,1,0:T(8,128)(2,1)S(1)} collective-permute-done((bf16[2,112,512]{2,1,0:T(8,128)(2,1)S(1)}, bf16[2,112,512]{2,1,0:T(8,128)(2,1)S(1)}, u32[]{:S(2)}, u32[]{:S(2)}) %collective-permute-start.74) | collective-permute-done | bytes 229408 | tf_op jit(solution)/shard_map/ppermute | solution.py:542
  (424 shorter events, 328.5 us)
Async XLA Ops:
  6.1 45.5 %all-to-all-start = ((bf16[8,112,1024]{2,1,0:T(8,128)(2,1)}), bf16[8,112,1024]{2,1,0:T(8,128)(2,1)S(1)}, u32[]{:S(2)}, u32[]{:S(2)}) async-start(bf16[8,112,1024]{2,1,0:T(8,128)(2,1)} %get-tuple-element.109), calls=%async_computation | async-start | bytes 3670016 | tf_op jit(solution)/shard_map/all_to_all | solution.py:253
  52.8 46.9 %all-to-all-start.1 = ((bf16[8,112,1024]{2,1,0:T(8,128)(2,1)}), bf16[8,112,1024]{2,1,0:T(8,128)(2,1)S(1)}, u32[]{:S(2)}, u32[]{:S(2)}) async-start(bf16[8,112,1024]{2,1,0:T(8,128)(2,1)} %get-tuple-element.114), calls=%async_computation.1 | async-start | bytes 3670016 | tf_op jit(solution)/shard_map/all_to_all | solution.py:253
  59.9 41.6 %collective-permute-start.3 = (bf16[896,1024]{1,0:T(8,128)(2,1)}, bf16[896,1024]{1,0:T(8,128)(2,1)}, u32[]{:S(2)}, u32[]{:S(2)}) collective-permute-start(bf16[896,1024]{1,0:T(8,128)(2,1)} %bitcast.254), channel_id=1, source_target_pairs={{0,8},{8,0},{16,24},{24,16},{1,9},{9,1},{17,25},{25,17},{2,10},{10... | collective-permute-start | bytes 5505032 | tf_op jit(solution)/shard_map/ppermute | solution.py:233
  61.1 41.2 %collective-permute-start.4 = (bf16[896,1024]{1,0:T(8,128)(2,1)}, bf16[896,1024]{1,0:T(8,128)(2,1)}, u32[]{:S(2)}, u32[]{:S(2)}) collective-permute-start(bf16[896,1024]{1,0:T(8,128)(2,1)} %bitcast.255), channel_id=1, source_target_pairs={{0,16},{8,24},{16,0},{24,8},{1,17},{9,25},{17,1},{25,9},{2,18},{10... | collective-permute-start | bytes 5505032 | tf_op jit(solution)/shard_map/ppermute | solution.py:233
  129.7 43.1 %collective-permute-start.11 = (bf16[3,112,896]{2,1,0:T(8,128)(2,1)S(1)}, bf16[3,112,896]{2,1,0:T(8,128)(2,1)S(1)}, u32[]{:S(2)}, u32[]{:S(2)}) collective-permute-start(bf16[3,112,896]{2,1,0:T(8,128)(2,1)S(1)} %pad_maximum_fusion.26), channel_id=1, source_target_pairs={{0,1},{1,0},{2,3},{3,2},{4,5},{5,4},{6,7},{7,6},{8,9},{9,8},{10,11... | collective-permute-start | bytes 1806344 | tf_op jit(solution)/shard_map/ppermute | solution.py:236
  176.0 32.0 %collective-permute-start.23 = (bf16[4,112,896]{2,1,0:T(8,128)(2,1)S(1)}, bf16[4,112,896]{2,1,0:T(8,128)(2,1)S(1)}, u32[]{:S(2)}, u32[]{:S(2)}) collective-permute-start(bf16[4,112,896]{2,1,0:T(8,128)(2,1)S(1)} %pad_maximum_fusion.18), channel_id=1, source_target_pairs={{0,1},{1,0},{2,3},{3,2},{4,5},{5,4},{6,7},{7,6},{8,9},{9,8},{10,11... | collective-permute-start | bytes 2408456 | tf_op jit(solution)/shard_map/ppermute | solution.py:236
  188.2 53.6 %collective-permute-start.24 = (bf16[4,112,896]{2,1,0:T(8,128)(2,1)S(1)}, bf16[4,112,896]{2,1,0:T(8,128)(2,1)S(1)}, u32[]{:S(2)}, u32[]{:S(2)}) collective-permute-start(bf16[4,112,896]{2,1,0:T(8,128)(2,1)S(1)} %pad_maximum_fusion.19), channel_id=1, source_target_pairs={{0,1},{1,0},{2,3},{3,2},{4,5},{5,4},{6,7},{7,6},{8,9},{9,8},{10,11... | collective-permute-start | bytes 2408456 | tf_op jit(solution)/shard_map/ppermute | solution.py:236
  208.3 32.1 %collective-permute-start.28 = (bf16[4,112,896]{2,1,0:T(8,128)(2,1)S(1)}, bf16[4,112,896]{2,1,0:T(8,128)(2,1)S(1)}, u32[]{:S(2)}, u32[]{:S(2)}) collective-permute-start(bf16[4,112,896]{2,1,0:T(8,128)(2,1)S(1)} %add_convert_fusion.2), channel_id=1, source_target_pairs={{0,2},{1,3},{2,4},{3,5},{4,6},{5,7},{6,0},{7,1},{8,10},{9,11},{10,... | collective-permute-start | bytes 2408456 | tf_op jit(solution)/shard_map/ppermute | solution.py:239
  241.3 44.1 %collective-permute-start.25 = (bf16[4,112,896]{2,1,0:T(8,128)(2,1)S(1)}, bf16[4,112,896]{2,1,0:T(8,128)(2,1)S(1)}, u32[]{:S(2)}, u32[]{:S(2)}) collective-permute-start(bf16[4,112,896]{2,1,0:T(8,128)(2,1)S(1)} %pad_maximum_fusion.20), channel_id=1, source_target_pairs={{0,1},{1,0},{2,3},{3,2},{4,5},{5,4},{6,7},{7,6},{8,9},{9,8},{10,11... | collective-permute-start | bytes 2408456 | tf_op jit(solution)/shard_map/ppermute | solution.py:236
  242.2 43.2 %collective-permute-start.34 = (bf16[4,112,896]{2,1,0:T(8,128)(2,1)S(1)}, bf16[4,112,896]{2,1,0:T(8,128)(2,1)S(1)}, u32[]{:S(2)}, u32[]{:S(2)}) collective-permute-start(bf16[4,112,896]{2,1,0:T(8,128)(2,1)S(1)} %add_convert_fusion.1), channel_id=1, source_target_pairs={{0,2},{1,3},{2,4},{3,5},{4,6},{5,7},{6,0},{7,1},{8,10},{9,11},{10,... | collective-permute-start | bytes 2408456 | tf_op jit(solution)/shard_map/ppermute | solution.py:239
  245.4 40.0 %collective-permute-start.35 = (bf16[3,112,896]{2,1,0:T(8,128)(2,1)S(1)}, bf16[3,112,896]{2,1,0:T(8,128)(2,1)S(1)}, u32[]{:S(2)}, u32[]{:S(2)}) collective-permute-start(bf16[3,112,896]{2,1,0:T(8,128)(2,1)S(1)} %collective-permute-done.29.refs_2_), channel_id=1, source_target_pairs={{0,2},{1,3},{2,4},{3,5},{4,6},{5,7},{6,0},{7,1},{8,10},{9,11},{10,... | collective-permute-start | bytes 1806344 | tf_op jit(solution)/shard_map/ppermute | solution.py:239
  285.9 43.7 %collective-permute-start.39 = (bf16[7,112,896]{2,1,0:T(8,128)(2,1)S(1)}, bf16[7,112,896]{2,1,0:T(8,128)(2,1)}, u32[]{:S(2)}, u32[]{:S(2)}) collective-permute-start(bf16[7,112,896]{2,1,0:T(8,128)(2,1)S(1)} %pad_maximum_fusion.15), channel_id=1, source_target_pairs={{0,1},{1,0},{2,3},{3,2},{4,5},{5,4},{6,7},{7,6},{8,9},{9,8},{10,11... | collective-permute-start | bytes 4214792 | tf_op jit(solution)/shard_map/ppermute | solution.py:236
  288.3 41.3 %collective-permute-start.41 = (bf16[3,112,896]{2,1,0:T(8,128)(2,1)S(1)}, bf16[3,112,896]{2,1,0:T(8,128)(2,1)S(1)}, u32[]{:S(2)}, u32[]{:S(2)}) collective-permute-start(bf16[3,112,896]{2,1,0:T(8,128)(2,1)S(1)} %collective-permute-done.35.refs_3_), channel_id=1, source_target_pairs={{0,2},{1,3},{2,4},{3,5},{4,6},{5,7},{6,0},{7,1},{8,10},{9,11},{10,... | collective-permute-start | bytes 1806344 | tf_op jit(solution)/shard_map/ppermute | solution.py:239
  365.6 42.3 %collective-permute-start.48 = (bf16[14,112,896]{2,1,0:T(8,128)(2,1)S(1)}, bf16[14,112,896]{2,1,0:T(8,128)(2,1)S(1)}, u32[]{:S(2)}, u32[]{:S(2)}) collective-permute-start(bf16[14,112,896]{2,1,0:T(8,128)(2,1)S(1)} %get-tuple-element.317), channel_id=1, source_target_pairs={{0,1},{1,0},{2,3},{3,2},{4,5},{5,4},{6,7},{7,6},{8,9},{9,8},{10,11... | collective-permute-start | bytes 8429576 | tf_op jit(solution)/shard_map/ppermute | solution.py:236
  366.8 41.0 %collective-permute-start.52 = (bf16[4,112,896]{2,1,0:T(8,128)(2,1)S(1)}, bf16[4,112,896]{2,1,0:T(8,128)(2,1)S(1)}, u32[]{:S(2)}, u32[]{:S(2)}) collective-permute-start(bf16[4,112,896]{2,1,0:T(8,128)(2,1)S(1)} %collective-permute-done.46.refs_3_), channel_id=1, source_target_pairs={{0,2},{1,3},{2,4},{3,5},{4,6},{5,7},{6,0},{7,1},{8,10},{9,11},{10,... | collective-permute-start | bytes 2408456 | tf_op jit(solution)/shard_map/ppermute | solution.py:239
  492.1 41.9 %collective-permute-start.64 = (bf16[2,896,512]{2,1,0:T(8,128)(2,1)}, bf16[2,896,512]{2,1,0:T(8,128)(2,1)S(1)}, u32[]{:S(2)}, u32[]{:S(2)}) collective-permute-start(bf16[2,896,512]{2,1,0:T(8,128)(2,1)} %bitcast.307), channel_id=1, source_target_pairs={{0,8},{8,0},{16,24},{24,16},{1,9},{9,1},{17,25},{25,17},{2,10},{10... | collective-permute-start | bytes 5505032 | tf_op jit(solution)/shard_map/ppermute | solution.py:233
  493.2 41.5 %collective-permute-start.65 = (bf16[2,896,512]{2,1,0:T(8,128)(2,1)}, bf16[2,896,512]{2,1,0:T(8,128)(2,1)S(1)}, u32[]{:S(2)}, u32[]{:S(2)}) collective-permute-start(bf16[2,896,512]{2,1,0:T(8,128)(2,1)} %bitcast.308), channel_id=1, source_target_pairs={{0,16},{8,24},{16,0},{24,8},{1,17},{9,25},{17,1},{25,9},{2,18},{10... | collective-permute-start | bytes 5505032 | tf_op jit(solution)/shard_map/ppermute | solution.py:233
  561.6 39.5 %collective-permute-start.68 = (bf16[2,896,512]{2,1,0:T(8,128)(2,1)}, bf16[2,896,512]{2,1,0:T(8,128)(2,1)}, u32[]{:S(2)}, u32[]{:S(2)}) collective-permute-start(bf16[2,896,512]{2,1,0:T(8,128)(2,1)} %bitcast.70), channel_id=1, source_target_pairs={{0,8},{8,0},{16,24},{24,16},{1,9},{9,1},{17,25},{25,17},{2,10},{10... | collective-permute-start | bytes 5505032 | tf_op jit(solution)/shard_map/ppermute | solution.py:233
  562.4 39.2 %collective-permute-start.69 = (bf16[2,896,512]{2,1,0:T(8,128)(2,1)}, bf16[2,896,512]{2,1,0:T(8,128)(2,1)}, u32[]{:S(2)}, u32[]{:S(2)}) collective-permute-start(bf16[2,896,512]{2,1,0:T(8,128)(2,1)} %bitcast.70), channel_id=1, source_target_pairs={{0,16},{8,24},{16,0},{24,8},{1,17},{9,25},{17,1},{25,9},{2,18},{10... | collective-permute-start | bytes 5505032 | tf_op jit(solution)/shard_map/ppermute | solution.py:233
  578.2 47.5 %all-to-all-start.2 = ((bf16[2,8,112,512]{3,2,0,1:T(8,128)(2,1)}), bf16[2,8,112,512]{3,2,0,1:T(8,128)(2,1)S(1)}, u32[]{:S(2)}, u32[]{:S(2)}) async-start(bf16[2,8,112,512]{3,2,0,1:T(8,128)(2,1)} %copy.85), calls=%async_computation.2 | async-start | bytes 3670016 | tf_op jit(solution)/shard_map/all_to_all | solution.py:519
  642.8 34.3 %collective-permute-start.74 = (bf16[2,112,512]{2,1,0:T(8,128)(2,1)S(1)}, bf16[2,112,512]{2,1,0:T(8,128)(2,1)S(1)}, u32[]{:S(2)}, u32[]{:S(2)}) collective-permute-start(bf16[2,112,512]{2,1,0:T(8,128)(2,1)S(1)} %get-tuple-element.258), channel_id=1, source_target_pairs={{0,3},{1,4},{2,5},{3,6},{4,7},{5,0},{6,1},{7,2},{8,11},{9,12},{10,... | collective-permute-start | bytes 688136 | tf_op jit(solution)/shard_map/ppermute | solution.py:542
  643.0 39.0 %collective-permute-start.75 = (bf16[2,112,512]{2,1,0:T(8,128)(2,1)S(1)}, bf16[2,112,512]{2,1,0:T(8,128)(2,1)S(1)}, u32[]{:S(2)}, u32[]{:S(2)}) collective-permute-start(bf16[2,112,512]{2,1,0:T(8,128)(2,1)S(1)} %get-tuple-element.257), channel_id=1, source_target_pairs={{0,4},{1,5},{2,6},{3,7},{4,0},{5,1},{6,2},{7,3},{8,12},{9,13},{10,... | collective-permute-start | bytes 688136 | tf_op jit(solution)/shard_map/ppermute | solution.py:542
  645.5 36.5 %collective-permute-start.76 = (bf16[2,112,512]{2,1,0:T(8,128)(2,1)S(1)}, bf16[2,112,512]{2,1,0:T(8,128)(2,1)S(1)}, u32[]{:S(2)}, u32[]{:S(2)}) collective-permute-start(bf16[2,112,512]{2,1,0:T(8,128)(2,1)S(1)} %get-tuple-element.256), channel_id=1, source_target_pairs={{0,5},{1,6},{2,7},{3,0},{4,1},{5,2},{6,3},{7,4},{8,13},{9,14},{10,... | collective-permute-start | bytes 688136 | tf_op jit(solution)/shard_map/ppermute | solution.py:542
  647.6 35.2 %collective-permute-start.77 = (bf16[2,112,512]{2,1,0:T(8,128)(2,1)S(1)}, bf16[2,112,512]{2,1,0:T(8,128)(2,1)S(1)}, u32[]{:S(2)}, u32[]{:S(2)}) collective-permute-start(bf16[2,112,512]{2,1,0:T(8,128)(2,1)S(1)} %get-tuple-element.255), channel_id=1, source_target_pairs={{0,6},{1,7},{2,0},{3,1},{4,2},{5,3},{6,4},{7,5},{8,14},{9,15},{10,... | collective-permute-start | bytes 688136 | tf_op jit(solution)/shard_map/ppermute | solution.py:542
  (132 other events, 1645.6 us)
